TPU v7x, 256 devices: a whole 4x4x8 slice. The times are simulated.
256 devices in a mesh: seq: 32 (over z, y), head: 8 (over x, core).
Axes of the slice: x: 4, y: 4, z: 8, core: 2. Of those that a mesh axis runs over, the one named last changes fastest.
Arguments:
- hidden: bfloat16 [2, 32768, 2048], P(None, 'seq'), may hold values from -6 to 6
- w_qkv: bfloat16 [2048, 2560], P(None, 'head')
- conv_weight: float32 [3, 2560], P(None, 'head'), may hold values from -1 to 1
- norm_gain: bfloat16 [2048], P('head'), may hold values from 0.5 to 1.5
- repo_lengths: int32 [2, 12], replicated, may hold values from 1 to 8192, 32768 in all within a row
Outputs:
- normed: bfloat16 [2, 32768, 2048], P(None, 'seq', 'head')
Inputs may be any that keep to these rules, and one draw needn't show every extreme that they name: `repo_lengths`: each row sums to 32768; the longest repository of every sequence has exactly 8192 tokens.
All inputs are finite; a program needn't handle non-finite values.
Results may differ from a plain program's by a relative error of at most 0.0085.
Values may be sent and summed in bfloat16 or wider, within the bound.
A program may use at most 128 MiB of HBM per device.

v0:
```python
import jax
import jax.numpy as jnp
from jax import lax
from jax.sharding import PartitionSpec as P

H = 16
FEAT = 16
HEAD = 128


def entering(shard, axis, combine, identity):
    count, place = (lax.axis_size(axis), lax.axis_index(axis))
    everything = jax.tree.map(
        lambda part, kind: lax.all_gather(part.astype(kind), axis),
        shard,
        (jnp.bfloat16, jnp.bfloat16, jnp.bfloat16),
    )
    start = jax.tree.map(
        lambda part, zero: jnp.broadcast_to(jnp.asarray(zero, part.dtype), part.shape),
        shard,
        identity,
    )

    def step(k, before):
        reached = k < place
        new = combine(
            before, jax.tree.map(lambda part, own: part[k].astype(own.dtype), everything, shard)
        )
        return jax.tree.map(lambda a, b: jnp.where(reached, a, b), new, before)

    return lax.fori_loop(0, count, step, start)


def from_behind(shard, axis, by):
    count = lax.axis_size(axis)
    pairs = [(i, i + by) for i in range(count) if 0 <= i + by < count]
    return lax.ppermute(shard, axis, pairs)


def features(values):
    first = values * FEAT ** (-0.25)
    outer = (values[..., :, None] * values[..., None, :]).reshape(
        values.shape[:-1] + (FEAT * FEAT,)
    )
    outer = outer * (1.0 / (2.0 * FEAT) ** 0.5)
    ones = jnp.ones(values.shape[:-1] + (1,), values.dtype)
    return jnp.concatenate([ones, first, outer], axis=-1)


def combine(earlier, later):
    early_flag, early_state, early_norm = earlier
    late_flag, late_state, late_norm = later
    keep_early = 1.0 - late_flag
    return (
        jnp.maximum(early_flag, late_flag),
        late_state + keep_early[:, None, None] * early_state,
        late_norm + keep_early[:, None, None] * early_norm,
    )


def prefix_states(flag, state, norm):
    identity = (jnp.zeros_like(flag), jnp.zeros_like(state), jnp.zeros_like(norm))
    result = entering((flag, state, norm), "seq", combine, identity)
    return (result[1], result[2])


def shards(hidden, w_qkv, conv_weight, norm_gain, repo_lengths):
    seqs_here, tok_rows, model_width = hidden.shape
    width = 2 * FEAT + HEAD
    heads_here = w_qkv.shape[1] // width
    taps = conv_weight.shape[0]
    margin = taps - 1
    qkv = jnp.dot(
        hidden.reshape(seqs_here * tok_rows, model_width), w_qkv, preferred_element_type=jnp.float32
    )
    qkv = qkv.astype(jnp.bfloat16).reshape(seqs_here, tok_rows, heads_here * width)
    rim = from_behind(qkv[:, tok_rows - margin :], "seq", 1)
    offset = lax.axis_index("seq") * tok_rows
    starts = jnp.cumsum(repo_lengths, axis=1) - repo_lengths
    places = offset + jnp.arange(-margin, tok_rows, dtype=jnp.int32)
    seg_ext = jnp.sum((starts[:, None, :] <= places[None, :, None]).astype(jnp.int32), axis=2) - 1
    segment = seg_ext[:, margin:]
    prev_seg = seg_ext[:, margin - 1]
    extended = jnp.concatenate([rim, qkv], axis=1).astype(jnp.float32)
    mixed = conv_weight[0] * extended[:, margin:]
    for back in range(1, taps):
        lower = margin - back
        same = seg_ext[:, lower : lower + tok_rows] == segment
        mixed = mixed + conv_weight[back] * jnp.where(
            same[..., None], extended[:, lower : lower + tok_rows], 0.0
        )
    mixed = mixed.astype(jnp.bfloat16).reshape(seqs_here, tok_rows, heads_here, width)
    phi_query = features(mixed[..., :FEAT].astype(jnp.float32)).astype(jnp.bfloat16)
    phi_key = features(mixed[..., FEAT : 2 * FEAT].astype(jnp.float32)).astype(jnp.bfloat16)
    values = mixed[..., 2 * FEAT :]
    phi_size = phi_query.shape[-1]
    block_rows = min(512, tok_rows)
    order = jnp.arange(block_rows, dtype=jnp.int32)
    causal = order[:, None] >= order[None, :]
    state = jnp.zeros((seqs_here, phi_size, heads_here, HEAD), jnp.float32)
    norm = jnp.zeros((seqs_here, heads_here, phi_size), jnp.float32)
    last_seg = prev_seg
    numer_parts = []
    denom_parts = []
    for block_index in range(tok_rows // block_rows):
        lower = block_index * block_rows
        query_block = phi_query[:, lower : lower + block_rows]
        key_block = phi_key[:, lower : lower + block_rows]
        value_block = values[:, lower : lower + block_rows]
        seg_block = segment[:, lower : lower + block_rows]
        scores = jnp.einsum(
            "bqhf,bkhf->bhqk", query_block, key_block, preferred_element_type=jnp.float32
        )
        allowed = causal[None] & (seg_block[:, :, None] == seg_block[:, None, :])
        scores = jnp.where(allowed[:, None], scores, 0.0)
        weights_low = scores.astype(jnp.bfloat16)
        numer = jnp.einsum(
            "bhqk,bkhv->bqhv", weights_low, value_block, preferred_element_type=jnp.float32
        )
        denom = jnp.transpose(jnp.sum(scores, axis=3), (0, 2, 1))
        use_carry = seg_block == last_seg[:, None]
        query_wide = query_block.astype(jnp.float32)
        carried = jnp.einsum("bqhf,bfhv->bqhv", query_wide, state, precision=lax.Precision.HIGHEST)
        carried_norm = jnp.einsum(
            "bqhf,bhf->bqh", query_wide, norm, precision=lax.Precision.HIGHEST
        )
        numer = numer + jnp.where(use_carry[:, :, None, None], carried, 0.0)
        denom = denom + jnp.where(use_carry[:, :, None], carried_norm, 0.0)
        block_tail = seg_block[:, -1]
        block_inside = seg_block == block_tail[:, None]
        masked_block = jnp.where(
            block_inside[:, :, None, None], key_block, jnp.zeros_like(key_block)
        )
        add_state = jnp.einsum(
            "bthf,bthv->bfhv", masked_block, value_block, preferred_element_type=jnp.float32
        )
        add_norm = jnp.sum(masked_block.astype(jnp.float32), axis=1)
        keep_old = block_tail == last_seg
        state = add_state + jnp.where(keep_old[:, None, None, None], state, 0.0)
        norm = add_norm + jnp.where(keep_old[:, None, None], norm, 0.0)
        last_seg = block_tail
        numer_parts.append(numer)
        denom_parts.append(denom)
    open_state = state.reshape(seqs_here, phi_size, heads_here * HEAD)
    open_flag = (last_seg != prev_seg).astype(jnp.float32)
    state_in, norm_in = prefix_states(open_flag, open_state, norm)
    numer_all = jnp.concatenate(numer_parts, axis=1)
    denom_all = jnp.concatenate(denom_parts, axis=1)
    query_all = phi_query.astype(jnp.float32)
    incoming = jnp.einsum(
        "bqhf,bfhv->bqhv",
        query_all,
        state_in.reshape(seqs_here, phi_size, heads_here, HEAD),
        precision=lax.Precision.HIGHEST,
    )
    incoming_norm = jnp.einsum("bqhf,bhf->bqh", query_all, norm_in, precision=lax.Precision.HIGHEST)
    use_in = segment == prev_seg[:, None]
    numer_all = numer_all + jnp.where(use_in[:, :, None, None], incoming, 0.0)
    denom_all = denom_all + jnp.where(use_in[:, :, None], incoming_norm, 0.0)
    attn = (numer_all / denom_all[..., None]).reshape(seqs_here, tok_rows, heads_here * HEAD)
    squares = jnp.sum(attn * attn, axis=-1)
    total = lax.psum(squares, "head")
    scale = lax.rsqrt(total / (H * HEAD) + 1e-06)
    return (attn * scale[..., None] * norm_gain.astype(jnp.float32)).astype(jnp.bfloat16)


def solution(mesh):
    in_specs = (P(None, "seq", None), P(None, "head"), P(None, "head"), P("head"), P())
    out_specs = P(None, "seq", "head")
    return jax.shard_map(shards, mesh=mesh, in_specs=in_specs, out_specs=out_specs, check_vma=False)
```

profile of v0, /device:TPU:1, one launch (start us, length us, event | category | flops | bytes accessed | tf_op | source)
XLA Modules:
  0.0 243.1 jit_solution(2050337650601752381)
XLA Ops:
  6.5 1.3 copy-done
  7.9 6.3 %convolution_convert_fusion = bf16[2048,320]{0,1:T(8,128)(2,1)S(1)} fusion(bf16[2048,2048]{1,0:T(8,128)(2,1)} %bitcast.94, bf16[2048,320]{0,1:T(8,128)(2,1)S(1)} %copy-done), kind=kOutput, calls=%fused_computation.16 | convolution fusion | flops 2685009920 | bytes 11010048 | tf_op jit(solution)/shard_map/dot_general | solution.py:73
  14.4 4.0 %collective-permute-start = (bf16[2,2,320]{1,2,0:T(8,128)(2,1)S(1)}, bf16[2,2,320]{1,2,0:T(8,128)(2,1)S(1)}, u32[]{:S(2)}, u32[]{:S(2)}) collective-permute-start(bf16[2,2,320]{1,2,0:T(8,128)(2,1)S(1)} %slice.99), channel_id=1, source_target_pairs={{0,8},{8,16},{16,24},{24,32},{32,40},{40,48},{48,56},{56,64},{64,7... | collective-permute-start | bytes 7688 | tf_op jit(solution)/shard_map/ppermute | solution.py:37
  19.4 1.9 collective-permute-done
  21.3 0.7 maximum_convert_fusion
  22.0 1.7 fusion.7
  23.7 1.3 multiply_convert_fusion
  25.1 2.8 %pad_maximum_fusion = (bf16[2,1024,2,273]{1,3,2,0:T(8,128)(2,1)}, bf16[2,1024,2,273]{1,3,2,0:T(8,128)(2,1)S(1)}) fusion(bf16[2,1024,2,256]{1,3,2,0:T(8,128)(2,1)S(1)} %bitcast.81, bf16[2,1024,2,16]{1,3,2,0:T(8,128)(2,1)S(1)} %get-tuple-element.213, bf16[273]{0:T(512)(128)(2,1)S(1)} %pad.7.clone, bf16[2,1024,2,256]{1,3,2,0:T(8,128)(2,1)S(1)} %bitcast.80, ...), kind=kLoop, calls=%fused_computation.25 | loop fusion | flops 12300288 | bytes 8929826 | tf_op jit(solution)/shard_map/concatenate | solution.py:47
  27.8 0.5 convolution_bitcast_fusion.1
  28.3 1.1 copy-done.5
  29.4 0.5 fusion.22
  30.1 1.3 reshape.189
  31.5 0.6 dynamic-slice
  33.1 65.0 %all-reduce = bf16[64]{0:T(256)(128)(2,1)S(1)} all-reduce(bf16[64]{0:T(256)(128)(2,1)S(1)} %dynamic-update-slice), channel_id=2, replica_groups=mesh['seq'=32,'head'=8] {'seq'}, use_global_device_ids=true, to_apply=%add | all-reduce | flops 64 | bytes 256
  98.4 0.9 compare_and_fusion.1
  99.3 2.5 %convert_reduce_fusion.1 = (f32[2,2,273]{2,1,0:T(2,128)S(1)}, f32[2,2,273]{2,1,0:T(2,128)S(1)}) fusion(bf16[2,1024,2,273]{1,3,2,0:T(8,128)(2,1)} %copy-done.3, pred[2,512]{1,0:T(4,128)(4,1)S(1)} %get-tuple-element.224, pred[2,512]{1,0:T(4,128)(4,1)S(1)} %get-tuple-element.220), kind=kLoop, calls=%fused_computation.28 | loop fusion | flops 3352440 | bytes 2247200 | tf_op jit(solution)/shard_map/reduce_sum | solution.py:137
  102.0 35.6 %all_gather.14 = bf16[32,2,2,273]{3,2,1,0:T(2,128)(2,1)S(1)} all-gather(bf16[1,2,2,273]{3,2,1,0:T(2,128)(2,1)S(1)} %fusion.49), channel_id=1, replica_groups=mesh['seq'=32,'head'=8] {'seq'}, dimensions={0}, use_global_device_ids=true | all-gather | bytes 72072 | tf_op jit(solution)/shard_map/all_gather | solution.py:14
  137.6 0.6 fusion.31
  138.2 1.5 select_reduce_fusion.1
  139.8 0.6 fusion.27
  140.4 1.5 select_reduce_fusion
  142.0 1.1 convolution_select_fusion.1
  143.1 1.1 convolution_select_fusion
  144.1 1.7 fusion.20
  145.8 1.6 fusion.18
  147.4 44.7 %while.16 = (s32[]{:T(128)}, f32[2,273,256]{2,1,0:T(8,128)S(1)}, f32[2,2,273]{2,1,0:T(2,128)S(1)}, s32[]{:T(128)}, bf16[32,2,273,256]{3,1,2,0:T(2,128)(2,1)}, /*...) while((s32[]{:T(128)}, f32[2,273,256]{2,1,0:T(8,128)S(1)}, ...), condition=%wide.region_5.6_spmd.clone, body=%wide.region_4.5_spmd.clone.sunk | while | flops 704348 | bytes 1967939 | solution.py:31
  147.5 1.2 constant_dynamic-slice_fusion.3
  148.9 1.2 constant_dynamic-slice_fusion.3
  150.3 1.2 constant_dynamic-slice_fusion.3
  151.6 1.2 constant_dynamic-slice_fusion.3
  153.0 1.2 constant_dynamic-slice_fusion.3
  154.4 1.2 constant_dynamic-slice_fusion.3
  155.8 1.2 constant_dynamic-slice_fusion.3
  157.2 1.2 constant_dynamic-slice_fusion.3
  158.6 1.2 constant_dynamic-slice_fusion.3
  160.0 1.2 constant_dynamic-slice_fusion.3
  161.4 1.2 constant_dynamic-slice_fusion.3
  162.8 1.2 constant_dynamic-slice_fusion.3
  164.2 1.2 constant_dynamic-slice_fusion.3
  165.6 1.2 constant_dynamic-slice_fusion.3
  167.0 1.2 constant_dynamic-slice_fusion.3
  168.4 1.2 constant_dynamic-slice_fusion.3
  169.8 1.2 constant_dynamic-slice_fusion.3
  171.2 1.2 constant_dynamic-slice_fusion.3
  172.6 1.2 constant_dynamic-slice_fusion.3
  174.0 1.2 constant_dynamic-slice_fusion.3
  175.4 1.2 constant_dynamic-slice_fusion.3
  176.8 1.2 constant_dynamic-slice_fusion.3
  178.2 1.2 constant_dynamic-slice_fusion.3
  179.6 1.2 constant_dynamic-slice_fusion.3
  181.0 1.2 constant_dynamic-slice_fusion.3
  182.4 1.2 constant_dynamic-slice_fusion.3
  183.8 1.2 constant_dynamic-slice_fusion.3
  185.2 1.2 constant_dynamic-slice_fusion.3
  186.6 1.2 constant_dynamic-slice_fusion.3
  188.0 1.2 constant_dynamic-slice_fusion.3
  189.4 1.2 constant_dynamic-slice_fusion.3
  190.8 1.2 constant_dynamic-slice_fusion.3
  192.2 0.3 reshape.170
  192.5 2.9 %fusion.50 = f32[2,2,1,1024]{3,2,1,0:T(1,128)S(1)} fusion(bf16[2,1024,2,273]{1,3,2,0:T(8,128)(2,1)} %get-tuple-element.228, f32[2,2,273,1]{2,1,0,3:T(2,128)S(1)} %bitcast.92), kind=kOutput, calls=%fused_computation.97 | convolution fusion | flops 13418496 | bytes 2257168 | tf_op jit(solution)/shard_map/bqhf,bhf->bqh/dot_general | solution.py:156
  195.5 4.9 %multiply_reduce_fusion = (f32[2,1024]{1,0:T(2,128)S(1)}, f32[2,1024,2,128]{1,3,2,0:T(8,128)}) fusion(f32[2,1024,2]{1,2,0:T(2,128)S(1)} %maximum_add_fusion.1, bf16[2,1024,2,273]{1,3,2,0:T(8,128)(2,1)S(1)} %copy-done.2, f32[2,273,2,128]{3,2,1,0:T(2,128)S(1)} %reshape.170, pred[2,1024]{1,0:T(4,128)(4,1)S(1)} %get-tuple-element.221, ...), kind=kOutput, calls=%fused_computation.34 | convolution fusion | flops 1720711168 | bytes 7016448 | tf_op jit(solution)/shard_map/bqhf,bfhv->bqhv/dot_general | solution.py:150
  200.4 1.9 copy.116
  202.3 32.6 %psum.7 = f32[2,1024]{1,0:T(2,128)S(1)} all-reduce(f32[2,1024]{1,0:T(2,128)S(1)} %get-tuple-element.234), channel_id=1, replica_groups=mesh['seq'=32,'head'=8] {'head'}, use_global_device_ids=true, to_apply=%region_9.10 | all-reduce | flops 2048 | bytes 16384 | tf_op jit(solution)/shard_map/psum | solution.py:162
  234.9 1.3 multiply_convert_fusion.2
  (150 shorter events, 9.6 us)
Async XLA Ops:
  6.5 1.3 copy-start
  6.5 140.9 %all-gather.3.cloned.1.call-start = ((), (), s32[]{:S(2)}) async-start(), calls=%async_computation | async-start | bytes 9225216 | tf_op jit(solution)/shard_map/all_gather | solution.py:14
  14.1 4.3 %copy-start.7 = (s32[2,12]{1,0:T(2,128)S(1)}, s32[2,12]{1,0:T(2,128)}, u32[]{:S(2)}) copy-start(s32[2,12]{1,0:T(2,128)} %param.11) | copy-start | bytes 292
  14.1 5.2 %copy-start.8 = (f32[3,320]{1,0:T(4,128)S(1)}, f32[3,320]{1,0:T(4,128)}, u32[]{:S(2)}) copy-start(f32[3,320]{1,0:T(4,128)} %param.9) | copy-start | bytes 11524
  14.4 6.9 %collective-permute-start = (bf16[2,2,320]{1,2,0:T(8,128)(2,1)S(1)}, bf16[2,2,320]{1,2,0:T(8,128)(2,1)S(1)}, u32[]{:S(2)}, u32[]{:S(2)}) collective-permute-start(bf16[2,2,320]{1,2,0:T(8,128)(2,1)S(1)} %slice.99), channel_id=1, source_target_pairs={{0,8},{8,16},{16,24},{24,32},{32,40},{40,48},{48,56},{56,64},{64,7... | collective-permute-start | bytes 7688 | tf_op jit(solution)/shard_map/ppermute | solution.py:37
  27.8 2.1 copy-start.3
  28.3 1.1 copy-start.5
  29.4 2.1 copy-start.10
  29.4 68.8 %copy-start.9 = (bf16[256]{0:T(256)(128)(2,1)S(1)}, bf16[256]{0:T(256)(128)(2,1)}, u32[]{:S(2)}) copy-start(bf16[256]{0:T(256)(128)(2,1)} %param.10) | copy-start | bytes 1540
  98.2 39.3 %copy-start.1 = (bf16[2,1024,2,273]{1,3,2,0:T(8,128)(2,1)S(1)}, bf16[2,1024,2,273]{1,3,2,0:T(8,128)(2,1)}, u32[]{:S(2)}) copy-start(bf16[2,1024,2,273]{1,3,2,0:T(8,128)(2,1)} %get-tuple-element.228) | copy-start | bytes 6709252
  98.4 39.8 %copy-start.4 = (bf16[2,1024,2,273]{1,3,2,0:T(8,128)(2,1)S(1)}, bf16[2,1024,2,273]{1,3,2,0:T(8,128)(2,1)}, u32[]{:S(2)}) copy-start(bf16[2,1024,2,273]{1,3,2,0:T(8,128)(2,1)} %copy-done.3) | copy-start | bytes 6709252
  142.0 1.1 copy-start.6
  192.5 3.0 %copy-start.2 = (bf16[2,1024,2,273]{1,3,2,0:T(8,128)(2,1)S(1)}, bf16[2,1024,2,273]{1,3,2,0:T(8,128)(2,1)}, u32[]{:S(2)}) copy-start(bf16[2,1024,2,273]{1,3,2,0:T(8,128)(2,1)} %get-tuple-element.228) | copy-start | bytes 6709252
Sparse Core Ops, SparseCore 0:
  31.6 107.3 all-gather.2
where the time goes:
time: 244 us; the launch traced here: 243 us
  blocking collectives  133 us (55%)
  local copies, waits for them, and re-layouts  44.7 us (18%)
  matrix products  24.9 us (10%)
  other arithmetic  19.4 us (8%)
  between operations  14.3 us (6%)
  starting transfers between devices  4.05 us (2%)
    unnamed x1, blocking collectives  65 us
    dynamic_slice x32, local copies, waits for them, and re-layouts, step(): part[k].astype(own.dtype)  36.9 us
    all_gather x1, blocking collectives, entering(): lax.all_gather(part.astype(kind), axis)  35.6 us
    psum x1, blocking collectives, shards(): total = lax.psum(squares, 'head')  32.6 us
    select_n x64, other arithmetic, step(): return jax.tree.map(lambda a, b: jnp.where(reached, a, b), new, before)  7.01 us
    dot_general x1, matrix products, shards(): jnp.dot(hidden.reshape(seqs_here * tok_rows, model_width), w_qkv, preferr...  6.28 us
    dot_general x1, matrix products, shards(): jnp.einsum('bqhf,bfhv->bqhv', query_all, state_in.reshape(seqs_here, phi_...  4.92 us
  transfers between devices with their start and end apart: 2, of which 1 were waited for; matrix products, arithmetic and copies ran while one was open for 6% of the time, Pallas kernels for 0%

commit v1 on v0

v1 whole, which is shorter than its diff:
```python
import functools
import jax
import jax.numpy as jnp
import numpy as np
from jax import lax
from jax.experimental import pallas as pl
from jax.experimental.pallas import tpu as pltpu
from jax.sharding import PartitionSpec as P

FEAT = 16
HEAD = 128
WIDTH = 2 * FEAT + HEAD
NSEG = 12
ROW = 4
CHUNK = 256
RIM = 16
KEPT = 160
PIECE = 80
ONE = 64
ZROW = 153
MESH = pl.DeviceIdType.MESH
bf16 = jnp.bfloat16
f32 = jnp.float32


def tables():
    pairs = [(0, i) for i in range(FEAT + 1)]
    pairs += [(i, j) for i in range(1, FEAT + 1) for j in range(i, FEAT + 1)]
    query = np.zeros((2, 128, 512), np.float32)
    key = np.zeros((2, 2 * KEPT, 128), np.float32)
    move = np.zeros((2, 128, 128), np.float32)
    for h in range(2):
        def lane(i, base):
            return ONE if i == 0 else base + i - 1
        qb, kb = 32 * h, 32 * h + FEAT
        for f, (i, j) in enumerate(pairs):
            if j == 0:
                sq, sk = 1.0, 1 / 8
            elif i == 0:
                sq, sk = 1 / 4, 1 / 8
            elif i == j:
                sq, sk = 1 / 16, 1 / 16
            else:
                sq, sk = 1 / 8, 1 / 16
            query[h, lane(i, qb), f] = sq
            query[h, lane(j, qb), 256 + f] = 1.0
            key[h, f, lane(i, kb)] = sk
            key[h, KEPT + f, lane(j, kb)] = 1.0
        for i in range(FEAT):
            move[h, kb + i, qb + i] = 1 / 16
        move[h, ONE, ONE] = 1 / 4
    return query.astype(jnp.bfloat16), key.astype(jnp.bfloat16), move.astype(jnp.bfloat16)


def nt(a, b):
    return lax.dot_general(a, b, (((1,), (1,)), ((), ())), preferred_element_type=f32)


def nn(a, b):
    return jnp.dot(a, b, preferred_element_type=f32)


def iota(shape, dim):
    return lax.broadcasted_iota(jnp.int32, shape, dim)


def kernel(zn, hn, hid, wq, conv, gain, lengths, eq, ek, mk, out,
           hbuf, wraw, wbuf, taps, qkv, lo, qk, kk, vv, phq, nd, att, rim_s, rim_r, lbuf, xbuf, rsend, zbuf,
           esend, ebuf, ssb, ssr, obuf,
           wsem, hsem, osem, rim_sem, p1s, p1r, p2s, p2r, p3s, p3r, sss, ssrs):
    T = hbuf.shape[1]
    C = T // CHUNK
    G = T // 128
    me = lax.axis_index("seq")
    hd = lax.axis_index("head")
    z = me // ROW
    y = lax.rem(me, ROW)

    def at_seq(i):
        return (i, hd)

    def along_y(k):
        return (z * ROW + lax.rem(y + k + ROW, ROW), hd)

    def along_z(k):
        return (lax.rem(z + k + zn, zn) * ROW + y, hd)

    def along_h(k):
        return (me, lax.rem(hd + k + hn, hn))

    nxt = at_seq(lax.rem(me + 1, zn * ROW))
    prv = at_seq(lax.rem(me + zn * ROW - 1, zn * ROW))

    wcopy = pltpu.make_async_copy(wq, wraw, wsem)
    wcopy.start()
    order = [(0, C - 1), (1, C - 1)] + [(0, c) for c in range(C - 1)] + [(1, c) for c in range(C - 1)]

    def fetch(s, c):
        rows = pl.ds(c * CHUNK, CHUNK)
        return pltpu.make_async_copy(hid.at[s, rows], hbuf.at[s, rows], hsem.at[s, c])

    for s, c in order:
        fetch(s, c).start()

    barrier = pltpu.get_barrier_semaphore()
    sources = [prv] + [along_y(-k) for k in (1, 2, 3)] + [along_z(-k) for k in (1, 2)]
    sources += [along_h(-k) for k in range(1, hn)]
    for d in sources:
        pl.semaphore_signal(barrier, inc=1, device_id=d, device_id_type=MESH)

    starts = []
    for s in range(2):
        run = jnp.int32(0)
        own = []
        for r in range(NSEG - 1):
            run = run + lengths[s, r]
            own.append(run)
        starts.append(own)

    def begin_of(s, t):
        found = jnp.int32(0)
        for b in starts[s]:
            found = jnp.where(b <= t, b, found)
        return found

    base = me * T

    for s in range(2):
        for r0 in range(0, T, 64):
            pos = base + r0 + iota((64, 128), 0)
            found = jnp.zeros((64, 128), jnp.int32)
            for b in starts[s]:
                found = jnp.where(pos >= b, b, found)
            lo[s, r0:r0 + 64, :] = found - base
        for h in range(2):
            vv[2 * s + h, :, HEAD:] = jnp.ones((T, HEAD), bf16)

    for j in range(3):
        row = conv[j:j + 1, :]
        taps[j:j + 1, 0:128] = row[:, 32:160]
        taps[j:j + 1, 128:256] = row[:, 192:320]
        taps[j:j + 1, 256:384] = jnp.concatenate(
            [row[:, 0:32], row[:, 160:192], jnp.zeros((1, 64), f32)], axis=1)

    wcopy.wait()
    D = wraw.shape[0]
    for r0 in range(0, D, 256):
        rows = slice(r0, r0 + 256)
        wbuf[rows, 0:128] = wraw[rows, 32:160]
        wbuf[rows, 128:256] = wraw[rows, 192:320]
        wbuf[rows, 256:384] = jnp.concatenate(
            [wraw[rows, 0:32], wraw[rows, 160:192], jnp.zeros((256, 64), bf16)], axis=1)

    def project(s, c):
        fetch(s, c).wait()
        low = nn(hbuf[s, c * CHUNK:(c + 1) * CHUNK, :], wbuf[...]).astype(bf16)
        qkv[s, RIM + c * CHUNK:RIM + (c + 1) * CHUNK, :] = low.astype(f32)
        if c == C - 1:
            rim_s[s] = low[CHUNK - RIM:, :]

    rim = pltpu.make_async_remote_copy(rim_s, rim_r, rim_sem.at[0], rim_sem.at[1], device_id=nxt, device_id_type=MESH)

    def mix(s, c):
        for r0 in range(c * CHUNK, (c + 1) * CHUNK, 64):
            first = lo[s, r0:r0 + 64, :]
            pos = r0 + iota((64, 128), 0)
            one_back = first < pos
            two_back = first < pos - 1
            for j in range(3):
                lanes = slice(128 * j, 128 * j + 128)
                x0 = qkv[s, RIM + r0:RIM + r0 + 64, lanes]
                x1 = qkv[s, RIM + r0 - 1:RIM + r0 + 63, lanes]
                x2 = qkv[s, RIM + r0 - 2:RIM + r0 + 62, lanes]
                m = taps[0:1, lanes] * x0
                m = m + taps[1:2, lanes] * jnp.where(one_back, x1, 0.0)
                m = m + taps[2:3, lanes] * jnp.where(two_back, x2, 0.0)
                if j < 2:
                    vv[2 * s + j, r0:r0 + 64, 0:HEAD] = m.astype(bf16)
                else:
                    m = jnp.where(iota((64, 128), 1) == ONE, 1.0, m)
                    qk[s, r0:r0 + 64, :] = m.astype(bf16)

    def summarise(s, h):
        g = 2 * s + h
        inside = begin_of(s, base + T - 1) - base
        total = jnp.zeros((KEPT, 2 * HEAD), f32)
        for c in range(C):
            rows = slice(c * CHUNK, (c + 1) * CHUNK)
            wide = nt(ek[h], qk[s, rows, :])
            phi = wide[:KEPT] * wide[KEPT:]
            phi = jnp.where(c * CHUNK + iota((KEPT, CHUNK), 1) >= inside, phi, 0.0).astype(bf16)
            total = total + nn(phi, vv[g, rows, :])
        state, norm = total[:, :HEAD], total[:, HEAD:]
        f, l = iota((KEPT, HEAD), 0), iota((KEPT, HEAD), 1)
        n0 = jnp.sum(jnp.where(f == l, norm, 0.0), axis=0, keepdims=True)
        n1 = jnp.sum(jnp.where(f == l + HEAD, norm, 0.0), axis=0, keepdims=True)
        state = jnp.where(f == ZROW, n0, jnp.where(f == ZROW + 1, n1, state)).astype(bf16)
        lbuf[s, 2 * h] = state[:PIECE]
        lbuf[s, 2 * h + 1] = state[PIECE:]

    def p1(s, k):
        return pltpu.make_async_remote_copy(
            lbuf.at[s, lax.rem(y + k, ROW)], xbuf.at[s, k - 1], p1s.at[s, k - 1], p1r.at[s, k - 1],
            device_id=along_y(k), device_id_type=MESH)

    def p2(s, k):
        return pltpu.make_async_remote_copy(
            rsend.at[s], zbuf.at[s, k - 1], p2s.at[s, k - 1], p2r.at[s, k - 1],
            device_id=along_z(k), device_id_type=MESH)

    def p3(s, k):
        return pltpu.make_async_remote_copy(
            esend.at[s, k - 1], ebuf.at[s, y], p3s.at[s, k - 1], p3r.at[s, k - 1],
            device_id=along_y(k), device_id_type=MESH)

    def p3_in(s, k):
        return pltpu.make_async_remote_copy(
            esend.at[s, k - 1], ebuf.at[s, lax.rem(y - k + ROW, ROW)], p3s.at[s, k - 1], p3r.at[s, k - 1],
            device_id=along_y(k), device_id_type=MESH)

    def ss(s, k):
        return pltpu.make_async_remote_copy(
            ssb.at[s], ssr.at[s, k - 1], sss.at[s, k - 1], ssrs.at[s, k - 1],
            device_id=along_h(k), device_id_type=MESH)

    rowbase = z * (ROW * T)

    def last_of(j):
        return rowbase + (j + 1) * T - 1

    def gathered(s):
        parts = [lbuf[s, y].astype(f32)]
        places = [y]
        for k in (1, 2, 3):
            parts.append(xbuf[s, k - 1].astype(f32))
            places.append(lax.rem(y - k + ROW, ROW))
        return parts, places

    def row_sum(s):
        for k in (1, 2, 3):
            p1(s, k).wait_recv()
        parts, places = gathered(s)
        begin = begin_of(s, last_of(ROW - 1))
        total = jnp.zeros((PIECE, HEAD), f32)
        for part, j in zip(parts, places):
            total = total + jnp.where(begin <= last_of(j), part, 0.0)
        rsend[s] = total.astype(bf16)
        for k in (1, 2):
            p2(s, k).start()

    def entering(s):
        for k in (1, 2):
            p2(s, k).wait_recv()
        parts, places = gathered(s)
        one, two = zbuf[s, 0].astype(f32), zbuf[s, 1].astype(f32)
        for k in (1, 2, 3, 0):
            target = lax.rem(y + k, ROW)
            begin = begin_of(s, rowbase + target * T)
            total = jnp.where(begin < rowbase, one, 0.0) + jnp.where(begin < rowbase - ROW * T, two, 0.0)
            for part, j in zip(parts, places):
                reach = jnp.where(j < target, last_of(j), -1)
                total = total + jnp.where(begin <= reach, part, 0.0)
            if k:
                esend[s, k - 1] = total.astype(bf16)
                p3(s, k).start()
            else:
                ebuf[s, y] = total.astype(bf16)

    def attend(s, h):
        g = 2 * s + h
        for c in range(C):
            rows = slice(c * CHUNK, (c + 1) * CHUNK)
            q = qk[s, rows, :]
            first = jnp.concatenate([lo[s, rows, :]] * (CHUNK // 128), axis=1)
            cols = iota((CHUNK, CHUNK), 1)
            parts = []
            for b in range(c + 1):
                u = nt(q, kk[g, b * CHUNK:(b + 1) * CHUNK, :])
                u = u * u + 0.0625
                keep = cols + b * CHUNK >= first
                if b == c:
                    keep = keep & (cols <= iota((CHUNK, CHUNK), 0))
                parts.append(jnp.where(keep, u, 0.0).astype(bf16))
            weights = parts[0] if c == 0 else jnp.concatenate(parts, axis=1)
            nd[g, rows, :] = nn(weights, vv[g, :(c + 1) * CHUNK, :])

    def queries(s, h):
        g = 2 * s + h
        for c in range(C):
            rows = slice(c * CHUNK, (c + 1) * CHUNK)
            ab = nn(qk[s, rows, :], eq[h])
            phq[g, rows, :] = (ab[:, :256] * ab[:, 256:]).astype(bf16)

    def keys(s, h):
        for c in range(C):
            rows = slice(c * CHUNK, (c + 1) * CHUNK)
            kk[2 * s + h, rows, :] = nn(qk[s, rows, :], mk[h]).astype(bf16)

    def finish(s):
        for k in (1, 2, 3):
            p3_in(s, k).wait_recv()
        rhs = []
        f, l = iota((KEPT, HEAD), 0), iota((KEPT, HEAD), 1)
        for h in range(2):
            state = jnp.concatenate([ebuf[s, 2 * h], ebuf[s, 2 * h + 1]], axis=0)
            wide = state.astype(f32)
            n0, n1 = wide[ZROW:ZROW + 1], wide[ZROW + 1:ZROW + 2]
            norm = jnp.sum(jnp.where(f == l, n0, 0.0) + jnp.where(f == l + HEAD, n1, 0.0), axis=1, keepdims=True)
            norm = jnp.broadcast_to(norm, (KEPT, HEAD)).astype(bf16)
            both = jnp.concatenate([state, norm], axis=1)
            rhs.append(jnp.concatenate([both, jnp.zeros((256 - KEPT, 256), bf16)], axis=0))
        eye = iota((128, 128), 0) == iota((128, 128), 1)
        for r0 in range(0, T, 128):
            rows = slice(r0, r0 + 128)
            use = lo[s, rows, :] < 0
            squares = jnp.zeros((128, 128), f32)
            for h in range(2):
                g = 2 * s + h
                came = nn(phq[g, rows, :], rhs[h])
                num = nd[g, rows, :HEAD] + jnp.where(use, came[:, :HEAD], 0.0)
                den = nd[g, rows, HEAD:] + jnp.where(use, came[:, HEAD:], 0.0)
                a = num / den
                att[s, rows, h * HEAD:(h + 1) * HEAD] = a
                squares = squares + a * a
            col = jnp.sum(squares, axis=1, keepdims=True)
            i = r0 // 128
            ssb[s, i:i + 1, :] = jnp.sum(jnp.where(eye, col, 0.0), axis=0, keepdims=True)
        for k in range(1, hn):
            ss(s, k).start()

    def write(s, c):
        rows = pl.ds(c * CHUNK, CHUNK)
        return pltpu.make_async_copy(obuf.at[s, rows], out.at[s, rows], osem.at[s, c])

    def scale(s):
        for k in range(1, hn):
            ss(s, k).wait_recv()
        total = ssb[s]
        for k in range(1, hn):
            total = total + ssr[s, k - 1]
        factor = lax.rsqrt(total / (hn * 2 * HEAD) + 1e-06)
        eye = iota((128, 128), 0) == iota((128, 128), 1)
        g = gain[...].astype(f32)
        for r0 in range(0, T, 128):
            i = r0 // 128
            rows = slice(r0, r0 + 128)
            col = jnp.sum(jnp.where(eye, factor[i:i + 1, :], 0.0), axis=1, keepdims=True)
            obuf[s, rows, :] = (att[s, rows, :] * col * g).astype(bf16)
            if (r0 + 128) % CHUNK == 0:
                write(s, r0 // CHUNK).start()

    project(0, C - 1)
    project(1, C - 1)
    pl.semaphore_wait(barrier, len(sources))
    rim.start()
    for c in range(C - 1):
        project(0, c)
    for c in range(1, C):
        mix(0, c)
    rim.wait_recv()
    for s in range(2):
        qkv[s, 0:RIM, :] = rim_r[s].astype(f32)
    mix(0, 0)
    for h in range(2):
        summarise(0, h)
    for k in (1, 2, 3):
        p1(0, k).start()
    for c in range(C - 1):
        project(1, c)
    for c in range(C):
        mix(1, c)
    for h in range(2):
        summarise(1, h)
    for k in (1, 2, 3):
        p1(1, k).start()
    row_sum(0)
    keys(0, 0)
    attend(0, 0)
    row_sum(1)
    keys(0, 1)
    attend(0, 1)
    entering(0)
    queries(0, 0)
    queries(0, 1)
    keys(1, 0)
    attend(1, 0)
    entering(1)
    queries(1, 0)
    queries(1, 1)
    keys(1, 1)
    attend(1, 1)
    finish(0)
    finish(1)
    scale(0)
    scale(1)
    for s in range(2):
        for c in range(C):
            write(s, c).wait()
    rim.wait_send()
    for s in range(2):
        for k in (1, 2, 3):
            p1(s, k).wait_send()
            p3(s, k).wait_send()
        for k in (1, 2):
            p2(s, k).wait_send()
        for k in range(1, hn):
            ss(s, k).wait_send()


def shards(zn, hn, hidden, w_qkv, conv_weight, norm_gain, repo_lengths):
    seqs, T, D = hidden.shape
    C = T // CHUNK
    query, key, move = tables()
    any_spec = pl.BlockSpec(memory_space=pl.ANY)
    vmem = pl.BlockSpec(memory_space=pltpu.VMEM)
    dma = pltpu.SemaphoreType.DMA
    return pl.pallas_call(
        functools.partial(kernel, zn, hn),
        out_shape=jax.ShapeDtypeStruct((seqs, T, 2 * HEAD), bf16),
        in_specs=[any_spec, any_spec, vmem, vmem, pl.BlockSpec(memory_space=pltpu.SMEM), vmem, vmem, vmem],
        out_specs=any_spec,
        scratch_shapes=[
            pltpu.VMEM((2, T, D), bf16),
            pltpu.VMEM((D, 2 * WIDTH), bf16),
            pltpu.VMEM((D, 384), bf16),
            pltpu.VMEM((8, 384), f32),
            pltpu.VMEM((2, RIM + T, 384), f32),
            pltpu.VMEM((2, T, 128), jnp.int32),
            pltpu.VMEM((2, T, 128), bf16),
            pltpu.VMEM((4, T, 128), bf16),
            pltpu.VMEM((4, T, 256), bf16),
            pltpu.VMEM((4, T, 256), bf16),
            pltpu.VMEM((4, T, 256), f32),
            pltpu.VMEM((2, T, 256), f32),
            pltpu.VMEM((2, RIM, 384), bf16),
            pltpu.VMEM((2, RIM, 384), bf16),
            pltpu.VMEM((2, ROW, PIECE, HEAD), bf16),
            pltpu.VMEM((2, 3, PIECE, HEAD), bf16),
            pltpu.VMEM((2, PIECE, HEAD), bf16),
            pltpu.VMEM((2, 2, PIECE, HEAD), bf16),
            pltpu.VMEM((2, 3, PIECE, HEAD), bf16),
            pltpu.VMEM((2, ROW, PIECE, HEAD), bf16),
            pltpu.VMEM((2, T // 128, 128), f32),
            pltpu.VMEM((2, max(hn - 1, 1), T // 128, 128), f32),
            pltpu.VMEM((2, T, 256), bf16),
            dma,
            dma((2, C)),
            dma((2, C)),
            dma((2,)),
            dma((2, 3)),
            dma((2, 3)),
            dma((2, 2)),
            dma((2, 2)),
            dma((2, 3)),
            dma((2, 3)),
            dma((2, max(hn - 1, 1))),
            dma((2, max(hn - 1, 1))),
        ],
        compiler_params=pltpu.CompilerParams(
            collective_id=0, has_side_effects=True, vmem_limit_bytes=60 * 1024 * 1024),
        name="packed_linear_attention",
    )(hidden, w_qkv, conv_weight, norm_gain.reshape(1, 2 * HEAD), repo_lengths,
      jnp.asarray(query), jnp.asarray(key), jnp.asarray(move))


def solution(mesh):
    zn, hn = mesh.shape["seq"] // ROW, mesh.shape["head"]
    in_specs = (P(None, "seq", None), P(None, "head"), P(None, "head"), P("head"), P())
    out_specs = P(None, "seq", "head")
    return jax.shard_map(
        functools.partial(shards, zn, hn), mesh=mesh, in_specs=in_specs, out_specs=out_specs, check_vma=False)
```

time: 244 us -> 46.5 us (0.19)
  blocking collectives: 133 us -> 0 us
  Pallas kernels: 0 us -> 40.3 us
  local copies, waits for them, and re-layouts: 44.7 us -> 6.04 us
  matrix products: 24.9 us -> 0 us
  other arithmetic: 19.4 us -> 0 us
  between operations: 14.3 us -> 0.01 us
  starting transfers between devices: 4.05 us -> 0 us
    unnamed x1 -> x0, blocking collectives: 65 us -> none
    pallas_call x0 -> x1, Pallas kernels: none -> 40.3 us  [shards(): pl.pallas_call(functools.partial(kernel, zn, hn), out_shape=jax.ShapeDtyp...]
    dynamic_slice x32 -> x0, local copies, waits for them, and re-layouts: 36.9 us -> none  [step(): part[k].astype(own.dtype)]
    all_gather x1 -> x0, blocking collectives: 35.6 us -> none  [entering(): lax.all_gather(part.astype(kind), axis)]
    psum x1 -> x0, blocking collectives: 32.6 us -> none  [shards(): total = lax.psum(squares, 'head')]
    dot_general x13 -> x0, matrix products: 24.9 us -> none  [the longest x1 6.28 us: shards(): jnp.dot(hidden.reshape(seqs_here * tok_rows, model_width), w_qkv, preferr...]
    select_n x64 -> x0, other arithmetic: 7.01 us -> none  [step(): return jax.tree.map(lambda a, b: jnp.where(reached, a, b), new, before)]
    ppermute x1 -> x0, starting transfers between devices: 4.05 us -> none  [from_behind(): return lax.ppermute(shard, axis, pairs)]
  transfers between devices with their start and end apart: 2 -> 0, of which waited for: 1 -> 0; matrix products, arithmetic and copies ran while one was open for 6% -> 0% of each run, Pallas kernels for 0% -> 0%
where the time goes in v1:
time: 46.5 us; the launch traced here: 46.3 us
  Pallas kernels  40.3 us (87%)
  local copies, waits for them, and re-layouts  6.04 us (13%)
    pallas_call x1, Pallas kernels, shards(): pl.pallas_call(functools.partial(kernel, zn, hn), out_shape=jax.ShapeDtyp...  40.3 us
    unnamed x2, local copies, waits for them, and re-layouts  4.82 us
    reshape x1, local copies, waits for them, and re-layouts, shards(): norm_gain.reshape(1, 2 * HEAD)  1.22 us

profile of v1, /device:TPU:1, one launch (start us, length us, event | category | flops | bytes accessed | tf_op | source)
XLA Modules:
  0.0 46.3 jit_solution(374561677825739126)
XLA Ops:
  0.0 1.2 %reshape.3.gain = bf16[1,256]{1,0:T(2,128)(2,1)} reshape(bf16[256]{0:T(256)(128)(2,1)} %param.11) | data formatting | bytes 1024 | tf_op jit(solution)/shard_map/reshape | solution.py:462
  1.2 2.6 %copy.9.wq = bf16[2048,320]{1,0:T(8,128)(2,1)} copy(bf16[2048,320]{0,1:T(8,128)(2,1)} %param.9) | data formatting | bytes 2621440 | tf_op args[1]
  3.8 40.3 %packed_linear_attention.1 = bf16[2,1024,256]{2,1,0:T(8,128)(2,1)} custom-call(bf16[2,1024,2048]{2,1,0:T(8,128)(2,1)} %hid.1, bf16[2048,320]{1,0:T(8,128)(2,1)} %copy.9.wq, f32[3,320]{1,0:T(4,128)} %conv.1, bf16[1,256]{1,0:T(2,128)(2,1)} %reshape.3.gain, s32[2,12]{1,0:T(2,128)} %lengths.1, bf16[2,128,512]{2,1,0:T(8,128)(2,1)} %constant.6.clone.eq, ...), custom_call_target="tpu_custom_call" | custom-call | tf_op jit(solution)/shard_map/packed_linear_attention/pallas_call | solution.py:417
  44.0 2.3 %copy.11 = bf16[2,1024,256]{2,1,0:T(8,128)(2,1)} copy(bf16[2,1024,256]{2,1,0:T(8,128)(2,1)} %packed_linear_attention.1) | data formatting | bytes 2097152

commit v2 on v1

--- a/solution.py
+++ b/solution.py
@@ -64,10 +64,10 @@
     return lax.broadcasted_iota(jnp.int32, shape, dim)
 
 
-def kernel(zn, hn, hid, wq, conv, gain, lengths, eq, ek, mk, out,
-           hbuf, wraw, wbuf, taps, qkv, lo, qk, kk, vv, phq, nd, att, rim_s, rim_r, lbuf, xbuf, rsend, zbuf,
+def kernel(zn, hn, hid, wq, conv_in, gain_in, lengths, eq_in, ek_in, mk_in, out,
+           hbuf, wbuf, conv, gain, eq, ek, mk, taps, qkv, lo, qk, kk, vv, phq, nd, att, rim_s, rim_r, lbuf, xbuf, rsend, zbuf,
            esend, ebuf, ssb, ssr, obuf,
-           wsem, hsem, osem, rim_sem, p1s, p1r, p2s, p2r, p3s, p3r, sss, ssrs):
+           wsem, csem, hsem, osem, rim_sem, p1s, p1r, p2s, p2r, p3s, p3r, sss, ssrs):
     T = hbuf.shape[1]
     C = T // CHUNK
     G = T // 128
@@ -91,16 +91,27 @@
     nxt = at_seq(lax.rem(me + 1, zn * ROW))
     prv = at_seq(lax.rem(me + zn * ROW - 1, zn * ROW))
 
-    wcopy = pltpu.make_async_copy(wq, wraw, wsem)
-    wcopy.start()
+    def columns(i):
+        source, target, many = ((32, 0, 128), (192, 128, 128), (0, 256, 32), (160, 288, 32))[i]
+        return pltpu.make_async_copy(wq.at[pl.ds(source, many)], wbuf.at[pl.ds(target, many)], wsem.at[i])
+
+    def small(i):
+        source, target = ((conv_in, conv), (gain_in, gain), (ek_in, ek), (mk_in, mk), (eq_in, eq))[i]
+        return pltpu.make_async_copy(source, target, csem.at[i])
+
+    for i in range(4):
+        columns(i).start()
     order = [(0, C - 1), (1, C - 1)] + [(0, c) for c in range(C - 1)] + [(1, c) for c in range(C - 1)]
 
     def fetch(s, c):
         rows = pl.ds(c * CHUNK, CHUNK)
         return pltpu.make_async_copy(hid.at[s, rows], hbuf.at[s, rows], hsem.at[s, c])
 
-    for s, c in order:
+    for n, (s, c) in enumerate(order):
         fetch(s, c).start()
+        if n == 1:
+            for i in range(5):
+                small(i).start()
 
     barrier = pltpu.get_barrier_semaphore()
     sources = [prv] + [along_y(-k) for k in (1, 2, 3)] + [along_z(-k) for k in (1, 2)]
@@ -135,25 +146,21 @@
         for h in range(2):
             vv[2 * s + h, :, HEAD:] = jnp.ones((T, HEAD), bf16)
 
-    for j in range(3):
-        row = conv[j:j + 1, :]
-        taps[j:j + 1, 0:128] = row[:, 32:160]
-        taps[j:j + 1, 128:256] = row[:, 192:320]
-        taps[j:j + 1, 256:384] = jnp.concatenate(
-            [row[:, 0:32], row[:, 160:192], jnp.zeros((1, 64), f32)], axis=1)
-
-    wcopy.wait()
-    D = wraw.shape[0]
-    for r0 in range(0, D, 256):
-        rows = slice(r0, r0 + 256)
-        wbuf[rows, 0:128] = wraw[rows, 32:160]
-        wbuf[rows, 128:256] = wraw[rows, 192:320]
-        wbuf[rows, 256:384] = jnp.concatenate(
-            [wraw[rows, 0:32], wraw[rows, 160:192], jnp.zeros((256, 64), bf16)], axis=1)
+    wbuf[320:384, :] = jnp.zeros((64, wbuf.shape[1]), bf16)
+
+    def ready():
+        for i in range(5):
+            small(i).wait()
+        for j in range(3):
+            row = conv[j:j + 1, :]
+            taps[j:j + 1, 0:128] = row[:, 32:160]
+            taps[j:j + 1, 128:256] = row[:, 192:320]
+            taps[j:j + 1, 256:384] = jnp.concatenate(
+                [row[:, 0:32], row[:, 160:192], jnp.zeros((1, 64), f32)], axis=1)
 
     def project(s, c):
         fetch(s, c).wait()
-        low = nn(hbuf[s, c * CHUNK:(c + 1) * CHUNK, :], wbuf[...]).astype(bf16)
+        low = nt(hbuf[s, c * CHUNK:(c + 1) * CHUNK, :], wbuf[...]).astype(bf16)
         qkv[s, RIM + c * CHUNK:RIM + (c + 1) * CHUNK, :] = low.astype(f32)
         if c == C - 1:
             rim_s[s] = low[CHUNK - RIM:, :]
@@ -340,7 +347,7 @@
             total = total + ssr[s, k - 1]
         factor = lax.rsqrt(total / (hn * 2 * HEAD) + 1e-06)
         eye = iota((128, 128), 0) == iota((128, 128), 1)
-        g = gain[...].astype(f32)
+        g = gain[...].astype(f32).reshape(1, 2 * HEAD)
         for r0 in range(0, T, 128):
             i = r0 // 128
             rows = slice(r0, r0 + 128)
@@ -349,62 +356,49 @@
             if (r0 + 128) % CHUNK == 0:
                 write(s, r0 // CHUNK).start()
 
-    project(0, C - 1)
-    project(1, C - 1)
-    pl.semaphore_wait(barrier, len(sources))
-    rim.start()
-    for c in range(C - 1):
-        project(0, c)
-    for c in range(1, C):
-        mix(0, c)
-    rim.wait_recv()
-    for s in range(2):
-        qkv[s, 0:RIM, :] = rim_r[s].astype(f32)
-    mix(0, 0)
-    for h in range(2):
-        summarise(0, h)
-    for k in (1, 2, 3):
-        p1(0, k).start()
-    for c in range(C - 1):
-        project(1, c)
-    for c in range(C):
-        mix(1, c)
-    for h in range(2):
-        summarise(1, h)
-    for k in (1, 2, 3):
-        p1(1, k).start()
-    row_sum(0)
-    keys(0, 0)
-    attend(0, 0)
-    row_sum(1)
-    keys(0, 1)
-    attend(0, 1)
-    entering(0)
-    queries(0, 0)
-    queries(0, 1)
-    keys(1, 0)
-    attend(1, 0)
-    entering(1)
-    queries(1, 0)
-    queries(1, 1)
-    keys(1, 1)
-    attend(1, 1)
-    finish(0)
-    finish(1)
-    scale(0)
-    scale(1)
-    for s in range(2):
-        for c in range(C):
-            write(s, c).wait()
-    rim.wait_send()
-    for s in range(2):
+    def columns_in():
+        for i in range(4):
+            columns(i).wait()
+
+    def greet():
+        pl.semaphore_wait(barrier, len(sources))
+
+    def rim_in():
+        rim.wait_recv()
+        for s in range(2):
+            qkv[s, 0:RIM, :] = rim_r[s].astype(f32)
+
+    def pieces_out(s):
         for k in (1, 2, 3):
-            p1(s, k).wait_send()
-            p3(s, k).wait_send()
-        for k in (1, 2):
-            p2(s, k).wait_send()
-        for k in range(1, hn):
-            ss(s, k).wait_send()
+            p1(s, k).start()
+
+    def drain():
+        for s in range(2):
+            for c in range(C):
+                write(s, c).wait()
+        rim.wait_send()
+        for s in range(2):
+            for k in (1, 2, 3):
+                p1(s, k).wait_send()
+                p3(s, k).wait_send()
+            for k in (1, 2):
+                p2(s, k).wait_send()
+            for k in range(1, hn):
+                ss(s, k).wait_send()
+
+    plan = [(columns_in,), (project, 0, C - 1), (project, 1, C - 1), (greet,), (rim.start,), (ready,)]
+    plan += [(project, 0, c) for c in range(C - 1)]
+    plan += [(mix, 0, c) for c in range(1, C)]
+    plan += [(rim_in,), (mix, 0, 0), (summarise, 0, 0), (summarise, 0, 1), (pieces_out, 0)]
+    plan += [(project, 1, c) for c in range(C - 1)]
+    plan += [(mix, 1, c) for c in range(C)]
+    plan += [(summarise, 1, 0), (summarise, 1, 1), (pieces_out, 1)]
+    plan += [(row_sum, 0), (keys, 0, 0), (attend, 0, 0), (row_sum, 1), (keys, 0, 1), (attend, 0, 1)]
+    plan += [(entering, 0), (queries, 0, 0), (queries, 0, 1), (keys, 1, 0), (attend, 1, 0)]
+    plan += [(entering, 1), (queries, 1, 0), (queries, 1, 1), (keys, 1, 1), (attend, 1, 1)]
+    plan += [(finish, 0), (finish, 1), (scale, 0), (scale, 1), (drain,)]
+    for step, *where in plan:
+        step(*where)
 
 
 def shards(zn, hn, hidden, w_qkv, conv_weight, norm_gain, repo_lengths):
@@ -412,17 +406,20 @@
     C = T // CHUNK
     query, key, move = tables()
     any_spec = pl.BlockSpec(memory_space=pl.ANY)
-    vmem = pl.BlockSpec(memory_space=pltpu.VMEM)
     dma = pltpu.SemaphoreType.DMA
     return pl.pallas_call(
         functools.partial(kernel, zn, hn),
         out_shape=jax.ShapeDtypeStruct((seqs, T, 2 * HEAD), bf16),
-        in_specs=[any_spec, any_spec, vmem, vmem, pl.BlockSpec(memory_space=pltpu.SMEM), vmem, vmem, vmem],
+        in_specs=[any_spec] * 4 + [pl.BlockSpec(memory_space=pltpu.SMEM)] + [any_spec] * 3,
         out_specs=any_spec,
         scratch_shapes=[
             pltpu.VMEM((2, T, D), bf16),
-            pltpu.VMEM((D, 2 * WIDTH), bf16),
-            pltpu.VMEM((D, 384), bf16),
+            pltpu.VMEM((384, D), bf16),
+            pltpu.VMEM(conv_weight.shape, f32),
+            pltpu.VMEM(norm_gain.shape, bf16),
+            pltpu.VMEM(query.shape, bf16),
+            pltpu.VMEM(key.shape, bf16),
+            pltpu.VMEM(move.shape, bf16),
             pltpu.VMEM((8, 384), f32),
             pltpu.VMEM((2, RIM + T, 384), f32),
             pltpu.VMEM((2, T, 128), jnp.int32),
@@ -443,7 +440,8 @@
             pltpu.VMEM((2, T // 128, 128), f32),
             pltpu.VMEM((2, max(hn - 1, 1), T // 128, 128), f32),
             pltpu.VMEM((2, T, 256), bf16),
-            dma,
+            dma((4,)),
+            dma((5,)),
             dma((2, C)),
             dma((2, C)),
             dma((2,)),
@@ -459,7 +457,7 @@
         compiler_params=pltpu.CompilerParams(
             collective_id=0, has_side_effects=True, vmem_limit_bytes=60 * 1024 * 1024),
         name="packed_linear_attention",
-    )(hidden, w_qkv, conv_weight, norm_gain.reshape(1, 2 * HEAD), repo_lengths,
+    )(hidden, w_qkv.T, conv_weight, norm_gain, repo_lengths,
       jnp.asarray(query), jnp.asarray(key), jnp.asarray(move))
 
 

time: 46.5 us -> 41.7 us (0.90)
  local copies, waits for them, and re-layouts: 6.04 us -> 2.26 us
  Pallas kernels: 40.3 us -> 39.3 us
    unnamed x2 -> x1, local copies, waits for them, and re-layouts: 4.82 us -> 2.26 us
    reshape x1 -> x0, local copies, waits for them, and re-layouts: 1.22 us -> none  [shards(): norm_gain.reshape(1, 2 * HEAD)]
    pallas_call x1, Pallas kernels: 40.3 us -> 39.3 us  [shards(): pl.pallas_call(functools.partial(kernel, zn, hn), out_shape=jax.ShapeDtyp...]
where the time goes in v2:
time: 41.7 us; the launch traced here: 41.5 us
  Pallas kernels  39.3 us (94%)
  local copies, waits for them, and re-layouts  2.26 us (5%)
    pallas_call x1, Pallas kernels, shards(): pl.pallas_call(functools.partial(kernel, zn, hn), out_shape=jax.ShapeDtyp...  39.3 us
    unnamed x1, local copies, waits for them, and re-layouts  2.26 us

profile of v2, /device:TPU:1, one launch (start us, length us, event | category | flops | bytes accessed | tf_op | source)
XLA Modules:
  0.0 41.5 jit_solution(16844124917476921587)
XLA Ops:
  0.0 39.3 %packed_linear_attention.1 = bf16[2,1024,256]{2,1,0:T(8,128)(2,1)} custom-call(bf16[2,1024,2048]{2,1,0:T(8,128)(2,1)} %hid.1, bf16[320,2048]{1,0:T(8,128)(2,1)} %bitcast.1, f32[3,320]{1,0:T(4,128)} %conv_in.1, bf16[256]{0:T(256)(128)(2,1)} %gain_in.1, s32[2,12]{1,0:T(2,128)} %lengths.1, bf16[2,128,512]{2,1,0:T(8,128)(2,1)} %constant.6.clone.eq_in, ...), custom_call_target="tpu_custom_call" | custom-call | tf_op jit(solution)/shard_map/packed_linear_attention/pallas_call | solution.py:410
  39.3 2.3 %copy.10 = bf16[2,1024,256]{2,1,0:T(8,128)(2,1)} copy(bf16[2,1024,256]{2,1,0:T(8,128)(2,1)} %packed_linear_attention.1) | data formatting | bytes 2097152

commit v3 on v2

v3 whole, which is shorter than its diff:
```python
import functools
import jax
import jax.numpy as jnp
import numpy as np
from jax import lax
from jax.experimental import pallas as pl
from jax.experimental.pallas import tpu as pltpu
from jax.sharding import PartitionSpec as P

FEAT = 16
HEAD = 128
WIDTH = 2 * FEAT + HEAD
NSEG = 12
ROW = 4
CHUNK = 256
RIM = 16
KEPT = 160
PIECE = 80
ONE = 64
QUAD = 136
ZROW = 137
LINEAR = 144
MESH = pl.DeviceIdType.MESH
bf16 = jnp.bfloat16
f32 = jnp.float32


def tables():
    query = np.zeros((2, 128, 512), np.float32)
    move = np.zeros((2, 128, 128), np.float32)
    for h in range(2):
        qb, kb = 32 * h, 32 * h + FEAT
        for f in range(QUAD):
            d, i = f // FEAT, f % FEAT
            query[h, qb + i, f] = 1 / 8 if d else 1 / 16
            query[h, qb + (i + d) % FEAT, 256 + f] = 1.0
        query[h, ONE, QUAD] = 1.0
        query[h, ONE, 256 + QUAD] = 1.0
        for i in range(FEAT):
            query[h, qb + i, LINEAR + i] = 1 / 4
            query[h, ONE, 256 + LINEAR + i] = 1.0
            move[h, qb + i, kb + i] = 1 / 16
        move[h, ONE, ONE] = 1 / 4
    return query.astype(jnp.bfloat16), move.astype(jnp.bfloat16)


def nt(a, b):
    return lax.dot_general(a, b, (((1,), (1,)), ((), ())), preferred_element_type=f32)


def nn(a, b):
    return jnp.dot(a, b, preferred_element_type=f32)


def iota(shape, dim):
    return lax.broadcasted_iota(jnp.int32, shape, dim)


def kernel(zn, hn, hid, wq, conv_in, lengths_in, eq_in, mk_in, att, fac,
           hbuf, wbuf, conv, lengths, eq, mk, taps, kd, qkv, lor, loc, qkt, qk, kk, vv, phq, nd, rim_s, rim_r, lbuf, xbuf,
           rsend, zbuf, esend, ebuf, ssb, ssr,
           wsem, csem, hsem, rim_sem, p1s, p1r, p2s, p2r, p3s, p3r, sss, ssrs):
    T = hbuf.shape[1]
    C = T // CHUNK
    G = T // 128
    me = lax.axis_index("seq")
    hd = lax.axis_index("head")
    z = me // ROW
    y = lax.rem(me, ROW)

    def at_seq(i):
        return (i, hd)

    def along_y(k):
        return (z * ROW + lax.rem(y + k + ROW, ROW), hd)

    def along_z(k):
        return (lax.rem(z + k + zn, zn) * ROW + y, hd)

    def along_h(k):
        return (me, lax.rem(hd + k + hn, hn))

    nxt = at_seq(lax.rem(me + 1, zn * ROW))
    prv = at_seq(lax.rem(me + zn * ROW - 1, zn * ROW))

    wcopy = pltpu.make_async_copy(wq, wbuf, wsem)

    def small(i):
        source, target = ((lengths_in, lengths), (conv_in, conv), (mk_in, mk), (eq_in, eq))[i]
        return pltpu.make_async_copy(source, target, csem.at[i])

    small(0).start()
    small(1).start()
    wcopy.start()
    order = [(0, C - 1), (1, C - 1)] + [(0, c) for c in range(C - 1)] + [(1, c) for c in range(C - 1)]

    def fetch(s, c):
        rows = pl.ds(c * CHUNK, CHUNK)
        return pltpu.make_async_copy(hid.at[s, rows], hbuf.at[s, rows], hsem.at[s, c])

    for n, (s, c) in enumerate(order):
        fetch(s, c).start()
        if n == 1:
            for i in range(2, 4):
                small(i).start()

    barrier = pltpu.get_barrier_semaphore()
    sources = [prv] + [along_y(-k) for k in (1, 2, 3)] + [along_z(-k) for k in (1, 2)]
    sources += [along_h(-k) for k in range(1, hn)]
    for d in sources:
        pl.semaphore_signal(barrier, inc=1, device_id=d, device_id_type=MESH)

    starts = []

    def bounds():
        small(0).wait()
        for s in range(2):
            run = jnp.int32(0)
            own = []
            for r in range(NSEG - 1):
                run = run + lengths[s, r]
                own.append(run)
            starts.append(own)

    def begin_of(s, t):
        found = jnp.int32(0)
        for b in starts[s]:
            found = jnp.where(b <= t, b, found)
        return found

    base = me * T

    def places(s, pos):
        found = jnp.zeros(pos.shape, jnp.int32)
        for b in starts[s]:
            found = jnp.where(pos >= b, b, found)
        return found - base

    def prepare():
        for s in range(2):
            lor[s] = places(s, base + iota((8, T), 1))
            qkt[s, ONE:ONE + 16, :] = jnp.where(iota((16, T), 0) == 0, 1.0, 0.0).astype(bf16)
            qkt[s, ONE + 16:, :] = jnp.zeros((128 - ONE - 16, T), bf16)
            for h in range(2):
                vv[2 * s + h, HEAD:, :] = jnp.ones((HEAD, T), bf16)
        small(1).wait()
        for j in range(3):
            for c0 in range(0, 2 * WIDTH, 64):
                row = jnp.broadcast_to(conv[j:j + 1, c0:c0 + 64], (64, 64))
                eye = iota((64, 64), 0) == iota((64, 64), 1)
                col = jnp.sum(jnp.where(eye, row, 0.0), axis=1, keepdims=True)
                taps[j, c0:c0 + 64, :] = jnp.broadcast_to(col, (64, 128))

    def ready():
        for i in range(2, 4):
            small(i).wait()

    def columns_in():
        wcopy.wait()

    def arrive(s, c):
        fetch(s, c).wait()

    def project(s, low_c, high_c):
        rows = slice(low_c * CHUNK, high_c * CHUNK)
        low = nt(wbuf[...], hbuf[s, rows, :]).astype(bf16)
        qkv[s, :, 128 + low_c * CHUNK:128 + high_c * CHUNK] = low.astype(f32)
        if high_c == C:
            pick = jnp.where(iota((RIM, 128), 1) == iota((RIM, 128), 0) + 128 - RIM, 1.0, 0.0).astype(bf16)
            rim_s[s] = nt(pick, low[:, low.shape[1] - 128:]).astype(bf16)

    rim = pltpu.make_async_remote_copy(rim_s, rim_r, rim_sem.at[0], rim_sem.at[1], device_id=nxt, device_id_type=MESH)

    def rim_in():
        rim.wait_recv()
        pick = jnp.where(iota((RIM, 128), 1) == iota((RIM, 128), 0) + 128 - RIM, 1.0, 0.0).astype(bf16)
        for s in range(2):
            qkv[s, :, 0:128] = lax.dot_general(
                rim_r[s], pick, (((0,), (0,)), ((), ())), preferred_element_type=f32)

    def mix(s, c):
        lanes = slice(c * CHUNK, (c + 1) * CHUNK)
        first = jnp.concatenate([lor[s, :, lanes]] * 4, axis=0)
        pos = c * CHUNK + iota((32, CHUNK), 1)
        one_back = first < pos
        two_back = first < pos - 1
        for r0 in range(0, 2 * WIDTH, 32):
            rows = slice(r0, r0 + 32)
            ext = qkv[s, rows, c * CHUNK:(c + 1) * CHUNK + 128]
            x1 = pltpu.roll(ext, 1, 1)[:, 128:]
            x2 = pltpu.roll(ext, 2, 1)[:, 128:]

            def tap(j):
                return jnp.concatenate([taps[j, rows, :]] * (CHUNK // 128), axis=1)

            m = tap(0) * ext[:, 128:]
            m = m + tap(1) * jnp.where(one_back, x1, 0.0)
            m = m + tap(2) * jnp.where(two_back, x2, 0.0)
            m = m.astype(bf16)
            h, d = r0 // WIDTH, r0 % WIDTH
            if d == 0:
                qkt[s, 32 * h:32 * h + 32, lanes] = m
            else:
                vv[2 * s + h, d - 32:d, lanes] = m

    def summarise(s):
        inside = begin_of(s, base + T - 1) - base
        for h in range(2):
            g = 2 * s + h
            key = qkt[s, 32 * h + FEAT:32 * h + 2 * FEAT, :].astype(f32)
            key = jnp.where(iota((FEAT, T), 1) >= inside, key, 0.0)
            small_key = key * (1.0 / 16.0)
            kd[g, 0:FEAT, :] = small_key
            kd[g, FEAT:2 * FEAT, :] = small_key
            blocks = [(key * kd[g, d:d + FEAT, :]).astype(bf16) for d in range(8)]
            here = (iota((8, T), 1) >= inside) & (iota((8, T), 0) == 0)
            last = [key[:8] * kd[g, 8:16, :], jnp.where(here, 0.125, 0.0)]
            blocks.append(jnp.concatenate(last, axis=0).astype(bf16))
            blocks.append((key * 0.125).astype(bf16))
            total = nt(jnp.concatenate(blocks, axis=0), vv[g])
            state, norm = total[:, :HEAD], total[:, HEAD:]
            f, l = iota((KEPT, HEAD), 0), iota((KEPT, HEAD), 1)
            n0 = jnp.sum(jnp.where(f == l, norm, 0.0), axis=0, keepdims=True)
            n1 = jnp.sum(jnp.where(f == l + HEAD, norm, 0.0), axis=0, keepdims=True)
            state = jnp.where(f == ZROW, n0, jnp.where(f == ZROW + 1, n1, state)).astype(bf16)
            lbuf[s, 2 * h] = state[:PIECE]
            lbuf[s, 2 * h + 1] = state[PIECE:]

    def p1(s, k):
        return pltpu.make_async_remote_copy(
            lbuf.at[s, lax.rem(y + k, ROW)], xbuf.at[s, k - 1], p1s.at[s, k - 1], p1r.at[s, k - 1],
            device_id=along_y(k), device_id_type=MESH)

    def p2(s, k):
        return pltpu.make_async_remote_copy(
            rsend.at[s], zbuf.at[s, k - 1], p2s.at[s, k - 1], p2r.at[s, k - 1],
            device_id=along_z(k), device_id_type=MESH)

    def p3(s, k):
        return pltpu.make_async_remote_copy(
            esend.at[s, k - 1], ebuf.at[s, y], p3s.at[s, k - 1], p3r.at[s, k - 1],
            device_id=along_y(k), device_id_type=MESH)

    def p3_in(s, k):
        return pltpu.make_async_remote_copy(
            esend.at[s, k - 1], ebuf.at[s, lax.rem(y - k + ROW, ROW)], p3s.at[s, k - 1], p3r.at[s, k - 1],
            device_id=along_y(k), device_id_type=MESH)

    def ss(s, k):
        return pltpu.make_async_remote_copy(
            ssb.at[s], ssr.at[s, k - 1], sss.at[s, k - 1], ssrs.at[s, k - 1],
            device_id=along_h(k), device_id_type=MESH)

    rowbase = z * (ROW * T)

    def last_of(j):
        return rowbase + (j + 1) * T - 1

    def gathered(s):
        parts = [lbuf[s, y].astype(f32)]
        owners = [y]
        for k in (1, 2, 3):
            parts.append(xbuf[s, k - 1].astype(f32))
            owners.append(lax.rem(y - k + ROW, ROW))
        return parts, owners

    def row_sum(s):
        for k in (1, 2, 3):
            p1(s, k).wait_recv()
        parts, owners = gathered(s)
        begin = begin_of(s, last_of(ROW - 1))
        total = jnp.zeros((PIECE, HEAD), f32)
        for part, j in zip(parts, owners):
            total = total + jnp.where(begin <= last_of(j), part, 0.0)
        rsend[s] = total.astype(bf16)
        for k in (1, 2):
            p2(s, k).start()

    def entering(s):
        for k in (1, 2):
            p2(s, k).wait_recv()
        parts, owners = gathered(s)
        one, two = zbuf[s, 0].astype(f32), zbuf[s, 1].astype(f32)
        for k in (1, 2, 3, 0):
            target = lax.rem(y + k, ROW)
            begin = begin_of(s, rowbase + target * T)
            total = jnp.where(begin < rowbase, one, 0.0) + jnp.where(begin < rowbase - ROW * T, two, 0.0)
            for part, j in zip(parts, owners):
                reach = jnp.where(j < target, last_of(j), -1)
                total = total + jnp.where(begin <= reach, part, 0.0)
            if k:
                esend[s, k - 1] = total.astype(bf16)
                p3(s, k).start()
            else:
                ebuf[s, y] = total.astype(bf16)

    def attend(s, h):
        g = 2 * s + h
        for c in range(C):
            rows = slice(c * CHUNK, (c + 1) * CHUNK)
            q = qk[s, rows, :]
            first = jnp.concatenate([loc[s, rows, :]] * (CHUNK // 128), axis=1)
            cols = iota((CHUNK, CHUNK), 1)
            parts = []
            for b in range(c + 1):
                u = nn(q, kk[g, :, b * CHUNK:(b + 1) * CHUNK])
                u = u * u + 0.0625
                keep = cols + b * CHUNK >= first
                if b == c:
                    keep = keep & (cols <= iota((CHUNK, CHUNK), 0))
                parts.append(jnp.where(keep, u, 0.0).astype(bf16))
            weights = parts[0] if c == 0 else jnp.concatenate(parts, axis=1)
            nd[g, rows, :] = nt(weights, vv[g, :, :(c + 1) * CHUNK])

    def queries(s, h):
        g = 2 * s + h
        for c in range(C):
            rows = slice(c * CHUNK, (c + 1) * CHUNK)
            ab = nn(qk[s, rows, :], eq[h])
            phq[g, rows, :] = (ab[:, :256] * ab[:, 256:]).astype(bf16)

    def turn(s):
        for r0 in range(0, T, 64):
            loc[s, r0:r0 + 64, :] = places(s, base + r0 + iota((64, 128), 0))
        same = jnp.where(iota((CHUNK, CHUNK), 0) == iota((CHUNK, CHUNK), 1), 1.0, 0.0).astype(bf16)
        for c in range(C):
            rows = slice(c * CHUNK, (c + 1) * CHUNK)
            qk[s, rows, :] = nt(same, qkt[s, :, rows]).astype(bf16)
        for h in range(2):
            kk[2 * s + h] = nn(mk[h], qkt[s]).astype(bf16)

    def finish(s):
        for k in (1, 2, 3):
            p3_in(s, k).wait_recv()
        rhs = []
        f, l = iota((KEPT, HEAD), 0), iota((KEPT, HEAD), 1)
        for h in range(2):
            state = jnp.concatenate([ebuf[s, 2 * h], ebuf[s, 2 * h + 1]], axis=0)
            wide = state.astype(f32)
            n0, n1 = wide[ZROW:ZROW + 1], wide[ZROW + 1:ZROW + 2]
            norm = jnp.sum(jnp.where(f == l, n0, 0.0) + jnp.where(f == l + HEAD, n1, 0.0), axis=1, keepdims=True)
            norm = jnp.broadcast_to(norm, (KEPT, HEAD)).astype(bf16)
            both = jnp.concatenate([state, norm], axis=1)
            rhs.append(jnp.concatenate([both, jnp.zeros((256 - KEPT, 256), bf16)], axis=0))
        eye = iota((128, 128), 0) == iota((128, 128), 1)
        for r0 in range(0, T, 128):
            rows = slice(r0, r0 + 128)
            use = loc[s, rows, :] < 0
            squares = jnp.zeros((128, 128), f32)
            for h in range(2):
                g = 2 * s + h
                came = nn(phq[g, rows, :], rhs[h])
                num = nd[g, rows, :HEAD] + jnp.where(use, came[:, :HEAD], 0.0)
                den = nd[g, rows, HEAD:] + jnp.where(use, came[:, HEAD:], 0.0)
                a = num / den
                att[s, rows, h * HEAD:(h + 1) * HEAD] = a
                squares = squares + a * a
            col = jnp.sum(squares, axis=1, keepdims=True)
            i = r0 // 128
            ssb[s, i:i + 1, :] = jnp.sum(jnp.where(eye, col, 0.0), axis=0, keepdims=True)
        for k in range(1, hn):
            ss(s, k).start()

    def scale(s):
        for k in range(1, hn):
            ss(s, k).wait_recv()
        total = ssb[s]
        for k in range(1, hn):
            total = total + ssr[s, k - 1]
        fac[s] = lax.rsqrt(total / (hn * 2 * HEAD) + 1e-06)

    def greet():
        pl.semaphore_wait(barrier, len(sources))

    def pieces_out(s):
        for k in (1, 2, 3):
            p1(s, k).start()

    def drain():
        rim.wait_send()
        for s in range(2):
            for k in (1, 2, 3):
                p1(s, k).wait_send()
                p3(s, k).wait_send()
            for k in (1, 2):
                p2(s, k).wait_send()
            for k in range(1, hn):
                ss(s, k).wait_send()

    plan = [(bounds,), (prepare,), (columns_in,), (arrive, 0, C - 1), (arrive, 1, C - 1)]
    plan += [(project, 0, C - 1, C), (project, 1, C - 1, C), (greet,), (rim.start,)]
    plan += [(arrive, 0, c) for c in range(C - 1)] + [(project, 0, 0, C - 1)]
    plan += [(arrive, 1, c) for c in range(C - 1)] + [(project, 1, 0, C - 1)]
    plan += [(mix, 0, c) for c in range(1, C)] + [(mix, 1, c) for c in range(1, C)]
    plan += [(rim_in,), (mix, 0, 0), (mix, 1, 0), (summarise, 0), (pieces_out, 0), (summarise, 1), (pieces_out, 1)]
    plan += [(ready,), (turn, 0), (turn, 1), (attend, 0, 0)]
    plan += [(row_sum, 0), (row_sum, 1), (attend, 0, 1), (attend, 1, 0)]
    plan += [(entering, 0), (entering, 1), (queries, 0, 0), (queries, 0, 1), (queries, 1, 0), (queries, 1, 1)]
    plan += [(attend, 1, 1), (finish, 0), (finish, 1), (scale, 0), (scale, 1), (drain,)]
    for step, *where in plan:
        step(*where)


def rescale(att, fac, gain, out, obuf, osem):
    T = att.shape[1]
    eye = iota((128, 128), 0) == iota((128, 128), 1)
    g = gain[...].astype(f32).reshape(1, 2 * HEAD)

    def write(s, c):
        rows = pl.ds(c * CHUNK, CHUNK)
        return pltpu.make_async_copy(obuf.at[s, rows], out.at[s, rows], osem.at[s, c])

    for s in range(2):
        for r0 in range(0, T, 128):
            i = r0 // 128
            rows = slice(r0, r0 + 128)
            col = jnp.sum(jnp.where(eye, fac[s, i:i + 1, :], 0.0), axis=1, keepdims=True)
            obuf[s, rows, :] = (att[s, rows, :] * col * g).astype(bf16)
            if (r0 + 128) % CHUNK == 0:
                write(s, r0 // CHUNK).start()
    for s in range(2):
        for c in range(T // CHUNK):
            write(s, c).wait()


def shards(zn, hn, hidden, w_qkv, conv_weight, norm_gain, repo_lengths):
    seqs, T, D = hidden.shape
    C = T // CHUNK
    query, move = tables()
    any_spec = pl.BlockSpec(memory_space=pl.ANY)
    vmem = pl.BlockSpec(memory_space=pltpu.VMEM)
    dma = pltpu.SemaphoreType.DMA

    def pin(x):
        return pltpu.with_memory_space_constraint(jnp.asarray(x), pltpu.HBM)

    att, fac = pl.pallas_call(
        functools.partial(kernel, zn, hn),
        out_shape=(jax.ShapeDtypeStruct((seqs, T, 2 * HEAD), f32), jax.ShapeDtypeStruct((seqs, T // 128, 128), f32)),
        in_specs=[any_spec] * 6,
        out_specs=(vmem, vmem),
        scratch_shapes=[
            pltpu.VMEM((2, T, D), bf16),
            pltpu.VMEM((2 * WIDTH, D), bf16),
            pltpu.VMEM(conv_weight.shape, f32),
            pltpu.SMEM(repo_lengths.shape, jnp.int32),
            pltpu.VMEM(query.shape, bf16),
            pltpu.VMEM(move.shape, bf16),
            pltpu.VMEM((3, 2 * WIDTH, 128), f32),
            pltpu.VMEM((4, 2 * FEAT, T), f32),
            pltpu.VMEM((2, 2 * WIDTH, 128 + T), f32),
            pltpu.VMEM((2, 8, T), jnp.int32),
            pltpu.VMEM((2, T, 128), jnp.int32),
            pltpu.VMEM((2, 128, T), bf16),
            pltpu.VMEM((2, T, 128), bf16),
            pltpu.VMEM((4, 128, T), bf16),
            pltpu.VMEM((4, 256, T), bf16),
            pltpu.VMEM((4, T, 256), bf16),
            pltpu.VMEM((4, T, 256), f32),
            pltpu.VMEM((2, RIM, 2 * WIDTH), bf16),
            pltpu.VMEM((2, RIM, 2 * WIDTH), bf16),
            pltpu.VMEM((2, ROW, PIECE, HEAD), bf16),
            pltpu.VMEM((2, 3, PIECE, HEAD), bf16),
            pltpu.VMEM((2, PIECE, HEAD), bf16),
            pltpu.VMEM((2, 2, PIECE, HEAD), bf16),
            pltpu.VMEM((2, 3, PIECE, HEAD), bf16),
            pltpu.VMEM((2, ROW, PIECE, HEAD), bf16),
            pltpu.VMEM((2, T // 128, 128), f32),
            pltpu.VMEM((2, max(hn - 1, 1), T // 128, 128), f32),
            dma,
            dma((4,)),
            dma((2, C)),
            dma((2,)),
            dma((2, 3)),
            dma((2, 3)),
            dma((2, 2)),
            dma((2, 2)),
            dma((2, 3)),
            dma((2, 3)),
            dma((2, max(hn - 1, 1))),
            dma((2, max(hn - 1, 1))),
        ],
        compiler_params=pltpu.CompilerParams(
            collective_id=0, has_side_effects=True, vmem_limit_bytes=44 * 1024 * 1024),
        name="packed_linear_attention",
    )(pin(hidden), pin(w_qkv.T), pin(conv_weight), pin(repo_lengths), pin(query), pin(move))
    return pl.pallas_call(
        rescale,
        out_shape=jax.ShapeDtypeStruct((seqs, T, 2 * HEAD), bf16),
        in_specs=[vmem, vmem, vmem],
        out_specs=any_spec,
        scratch_shapes=[pltpu.VMEM((2, T, 2 * HEAD), bf16), dma((2, C))],
        compiler_params=pltpu.CompilerParams(vmem_limit_bytes=8 * 1024 * 1024),
        name="rescale_rows",
    )(att, fac, norm_gain)


def solution(mesh):
    zn, hn = mesh.shape["seq"] // ROW, mesh.shape["head"]
    in_specs = (P(None, "seq", None), P(None, "head"), P(None, "head"), P("head"), P())
    out_specs = P(None, "seq", "head")
    return jax.shard_map(
        functools.partial(shards, zn, hn), mesh=mesh, in_specs=in_specs, out_specs=out_specs, check_vma=False)
```

time: 41.7 us -> 36.6 us (0.88)
  Pallas kernels: 39.3 us -> 36.5 us
  local copies, waits for them, and re-layouts: 2.26 us -> 0.01 us
    pallas_call x1 -> x2, Pallas kernels: 39.3 us -> 36.5 us  [the longest x1 35.4 us: shards(): pl.pallas_call(functools.partial(kernel, zn, hn), out_shape=(jax.ShapeDty...]
    unnamed x1 -> x2, local copies, waits for them, and re-layouts: 2.26 us -> 0.01 us
where the time goes in v3:
time: 36.6 us; the launch traced here: 36.5 us
  Pallas kernels  36.5 us (100%)
    pallas_call x1, Pallas kernels, shards(): pl.pallas_call(functools.partial(kernel, zn, hn), out_shape=(jax.ShapeDty...  35.4 us
    pallas_call x1, Pallas kernels, shards(): pl.pallas_call(rescale, out_shape=jax.ShapeDtypeStruct((seqs, T, 2 * HEAD...  1.14 us

profile of v3, /device:TPU:1, one launch (start us, length us, event | category | flops | bytes accessed | tf_op | source)
XLA Modules:
  0.0 36.5 jit_solution(14648064880187047635)
XLA Ops:
  0.0 0.0 copy-start
  0.0 35.4 %packed_linear_attention.1 = (f32[2,1024,256]{2,1,0:T(8,128)S(1)}, f32[2,8,128]{2,1,0:T(8,128)S(1)}) custom-call(bf16[2,1024,2048]{2,1,0:T(8,128)(2,1)} %hid.1, bf16[320,2048]{1,0:T(8,128)(2,1)} %bitcast.1, f32[3,320]{1,0:T(4,128)} %conv_in.1, s32[2,12]{1,0:T(2,128)} %lengths_in.1, bf16[2,128,512]{2,1,0:T(8,128)(2,1)} %constant.4.clone.eq_in, ...), custom_call_target="tpu_custom_call" | custom-call | tf_op jit(solution)/shard_map/packed_linear_attention/pallas_call | solution.py:437
  35.4 0.0 copy-done
  35.4 1.1 %rescale_rows.1 = bf16[2,1024,256]{2,1,0:T(8,128)(2,1)} custom-call(f32[2,1024,256]{2,1,0:T(8,128)S(1)} %get-tuple-element.7.att, f32[2,8,128]{2,1,0:T(8,128)S(1)} %get-tuple-element.8.fac, bf16[256]{0:T(256)(128)(2,1)S(1)} %copy-done), custom_call_target="tpu_custom_call" | custom-call | tf_op jit(solution)/shard_map/rescale_rows/pallas_call | solution.py:487
Async XLA Ops:
  0.0 35.4 %copy-start = (bf16[256]{0:T(256)(128)(2,1)S(1)}, bf16[256]{0:T(256)(128)(2,1)}, u32[]{:S(2)}) copy-start(bf16[256]{0:T(256)(128)(2,1)} %gain.1) | copy-start | bytes 1540

commit v4 on v3

--- a/solution.py
+++ b/solution.py
@@ -57,7 +57,7 @@
 
 
 def kernel(zn, hn, hid, wq, conv_in, lengths_in, eq_in, mk_in, att, fac,
-           hbuf, wbuf, conv, lengths, eq, mk, taps, kd, qkv, lor, loc, qkt, qk, kk, vv, phq, nd, rim_s, rim_r, lbuf, xbuf,
+           hbuf, wbuf, conv, lengths, eq, mk, taps, kd, partial, qkv, lor, loc, qkt, qk, kk, vv, phq, nd, rim_s, rim_r, lbuf, xbuf,
            rsend, zbuf, esend, ebuf, ssb, ssr,
            wsem, csem, hsem, rim_sem, p1s, p1r, p2s, p2r, p3s, p3r, sss, ssrs):
     T = hbuf.shape[1]
@@ -92,17 +92,15 @@
     small(0).start()
     small(1).start()
     wcopy.start()
-    order = [(0, C - 1), (1, C - 1)] + [(0, c) for c in range(C - 1)] + [(1, c) for c in range(C - 1)]
-
     def fetch(s, c):
         rows = pl.ds(c * CHUNK, CHUNK)
         return pltpu.make_async_copy(hid.at[s, rows], hbuf.at[s, rows], hsem.at[s, c])
 
-    for n, (s, c) in enumerate(order):
+    def request(s, c):
         fetch(s, c).start()
-        if n == 1:
-            for i in range(2, 4):
-                small(i).start()
+
+    request(0, C - 1)
+    request(1, C - 1)
 
     barrier = pltpu.get_barrier_semaphore()
     sources = [prv] + [along_y(-k) for k in (1, 2, 3)] + [along_z(-k) for k in (1, 2)]
@@ -155,6 +153,10 @@
         for i in range(2, 4):
             small(i).wait()
 
+    def tables_in():
+        for i in range(2, 4):
+            small(i).start()
+
     def columns_in():
         wcopy.wait()
 
@@ -203,21 +205,28 @@
             else:
                 vv[2 * s + h, d - 32:d, lanes] = m
 
-    def summarise(s):
+    def summarise(s, half):
         inside = begin_of(s, base + T - 1) - base
+        W = T // 2
+        at = half * W
+        lanes = slice(at, at + W)
         for h in range(2):
             g = 2 * s + h
-            key = qkt[s, 32 * h + FEAT:32 * h + 2 * FEAT, :].astype(f32)
-            key = jnp.where(iota((FEAT, T), 1) >= inside, key, 0.0)
+            key = qkt[s, 32 * h + FEAT:32 * h + 2 * FEAT, lanes].astype(f32)
+            key = jnp.where(at + iota((FEAT, W), 1) >= inside, key, 0.0)
             small_key = key * (1.0 / 16.0)
-            kd[g, 0:FEAT, :] = small_key
-            kd[g, FEAT:2 * FEAT, :] = small_key
-            blocks = [(key * kd[g, d:d + FEAT, :]).astype(bf16) for d in range(8)]
-            here = (iota((8, T), 1) >= inside) & (iota((8, T), 0) == 0)
-            last = [key[:8] * kd[g, 8:16, :], jnp.where(here, 0.125, 0.0)]
+            kd[g, 0:FEAT, lanes] = small_key
+            kd[g, FEAT:2 * FEAT, lanes] = small_key
+            blocks = [(key * kd[g, d:d + FEAT, lanes]).astype(bf16) for d in range(8)]
+            here = (at + iota((8, W), 1) >= inside) & (iota((8, W), 0) == 0)
+            last = [key[:8] * kd[g, 8:16, lanes], jnp.where(here, 0.125, 0.0)]
             blocks.append(jnp.concatenate(last, axis=0).astype(bf16))
             blocks.append((key * 0.125).astype(bf16))
-            total = nt(jnp.concatenate(blocks, axis=0), vv[g])
+            total = nt(jnp.concatenate(blocks, axis=0), vv[g, :, lanes])
+            if half == 0:
+                partial[g] = total
+                continue
+            total = partial[g] + total
             state, norm = total[:, :HEAD], total[:, HEAD:]
             f, l = iota((KEPT, HEAD), 0), iota((KEPT, HEAD), 1)
             n0 = jnp.sum(jnp.where(f == l, norm, 0.0), axis=0, keepdims=True)
@@ -387,12 +396,15 @@
             for k in range(1, hn):
                 ss(s, k).wait_send()
 
-    plan = [(bounds,), (prepare,), (columns_in,), (arrive, 0, C - 1), (arrive, 1, C - 1)]
-    plan += [(project, 0, C - 1, C), (project, 1, C - 1, C), (greet,), (rim.start,)]
-    plan += [(arrive, 0, c) for c in range(C - 1)] + [(project, 0, 0, C - 1)]
-    plan += [(arrive, 1, c) for c in range(C - 1)] + [(project, 1, 0, C - 1)]
+    L = C - 1
+    plan = [(bounds,), (prepare,), (columns_in,)] + [(request, 0, c) for c in range(L)]
+    plan += [(arrive, 0, L), (arrive, 1, L)] + [(request, 1, c) for c in range(L)] + [(tables_in,)]
+    plan += [(project, 0, L, C), (project, 1, L, C), (greet,), (rim.start,)]
+    plan += [(arrive, 0, c) for c in range(L)] + [(project, 0, 0, L)]
+    plan += [(arrive, 1, c) for c in range(L)] + [(project, 1, 0, L)]
     plan += [(mix, 0, c) for c in range(1, C)] + [(mix, 1, c) for c in range(1, C)]
-    plan += [(rim_in,), (mix, 0, 0), (mix, 1, 0), (summarise, 0), (pieces_out, 0), (summarise, 1), (pieces_out, 1)]
+    plan += [(rim_in,), (mix, 0, 0), (summarise, 0, 0), (summarise, 0, 1), (pieces_out, 0)]
+    plan += [(mix, 1, 0), (summarise, 1, 0), (summarise, 1, 1), (pieces_out, 1)]
     plan += [(ready,), (turn, 0), (turn, 1), (attend, 0, 0)]
     plan += [(row_sum, 0), (row_sum, 1), (attend, 0, 1), (attend, 1, 0)]
     plan += [(entering, 0), (entering, 1), (queries, 0, 0), (queries, 0, 1), (queries, 1, 0), (queries, 1, 1)]
@@ -448,6 +460,7 @@
             pltpu.VMEM(move.shape, bf16),
             pltpu.VMEM((3, 2 * WIDTH, 128), f32),
             pltpu.VMEM((4, 2 * FEAT, T), f32),
+            pltpu.VMEM((4, KEPT, 256), f32),
             pltpu.VMEM((2, 2 * WIDTH, 128 + T), f32),
             pltpu.VMEM((2, 8, T), jnp.int32),
             pltpu.VMEM((2, T, 128), jnp.int32),

time: 36.6 us -> 35 us (0.956)
  Pallas kernels: 36.5 us -> 34.9 us
    pallas_call x1, Pallas kernels: 35.4 us -> 33.8 us  [shards(): pl.pallas_call(functools.partial(kernel, zn, hn), out_shape=(jax.ShapeDty...]
where the time goes in v4:
time: 35 us; the launch traced here: 34.9 us
  Pallas kernels  34.9 us (100%)
    pallas_call x1, Pallas kernels, shards(): pl.pallas_call(functools.partial(kernel, zn, hn), out_shape=(jax.ShapeDty...  33.8 us
    pallas_call x1, Pallas kernels, shards(): pl.pallas_call(rescale, out_shape=jax.ShapeDtypeStruct((seqs, T, 2 * HEAD...  1.14 us

profile of v4, /device:TPU:1, one launch (start us, length us, event | category | flops | bytes accessed | tf_op | source)
XLA Modules:
  0.0 34.9 jit_solution(13996788694772298495)
XLA Ops:
  0.0 0.0 copy-start
  0.0 33.8 %packed_linear_attention.1 = (f32[2,1024,256]{2,1,0:T(8,128)S(1)}, f32[2,8,128]{2,1,0:T(8,128)S(1)}) custom-call(bf16[2,1024,2048]{2,1,0:T(8,128)(2,1)} %hid.1, bf16[320,2048]{1,0:T(8,128)(2,1)} %bitcast.1, f32[3,320]{1,0:T(4,128)} %conv_in.1, s32[2,12]{1,0:T(2,128)} %lengths_in.1, bf16[2,128,512]{2,1,0:T(8,128)(2,1)} %constant.4.clone.eq_in, ...), custom_call_target="tpu_custom_call" | custom-call | tf_op jit(solution)/shard_map/packed_linear_attention/pallas_call | solution.py:449
  33.8 0.0 copy-done
  33.8 1.1 %rescale_rows.1 = bf16[2,1024,256]{2,1,0:T(8,128)(2,1)} custom-call(f32[2,1024,256]{2,1,0:T(8,128)S(1)} %get-tuple-element.7.att, f32[2,8,128]{2,1,0:T(8,128)S(1)} %get-tuple-element.8.fac, bf16[256]{0:T(256)(128)(2,1)S(1)} %copy-done), custom_call_target="tpu_custom_call" | custom-call | tf_op jit(solution)/shard_map/rescale_rows/pallas_call | solution.py:500
Async XLA Ops:
  0.0 33.8 %copy-start = (bf16[256]{0:T(256)(128)(2,1)S(1)}, bf16[256]{0:T(256)(128)(2,1)}, u32[]{:S(2)}) copy-start(bf16[256]{0:T(256)(128)(2,1)} %gain.1) | copy-start | bytes 1540

commit v5 on v4

--- a/solution.py
+++ b/solution.py
@@ -58,7 +58,7 @@
 
 def kernel(zn, hn, hid, wq, conv_in, lengths_in, eq_in, mk_in, att, fac,
            hbuf, wbuf, conv, lengths, eq, mk, taps, kd, partial, qkv, lor, loc, qkt, qk, kk, vv, phq, nd, rim_s, rim_r, lbuf, xbuf,
-           rsend, zbuf, esend, ebuf, ssb, ssr,
+           rsend, zbuf, esend, ebuf, inrow, ssb, ssr,
            wsem, csem, hsem, rim_sem, p1s, p1r, p2s, p2r, p3s, p3r, sss, ssrs):
     T = hbuf.shape[1]
     C = T // CHUNK
@@ -232,76 +232,87 @@
             n0 = jnp.sum(jnp.where(f == l, norm, 0.0), axis=0, keepdims=True)
             n1 = jnp.sum(jnp.where(f == l + HEAD, norm, 0.0), axis=0, keepdims=True)
             state = jnp.where(f == ZROW, n0, jnp.where(f == ZROW + 1, n1, state)).astype(bf16)
-            lbuf[s, 2 * h] = state[:PIECE]
-            lbuf[s, 2 * h + 1] = state[PIECE:]
-
-    def p1(s, k):
+            lbuf[2 * h, s] = state[:PIECE]
+            lbuf[2 * h + 1, s] = state[PIECE:]
+
+    def p1(k):
         return pltpu.make_async_remote_copy(
-            lbuf.at[s, lax.rem(y + k, ROW)], xbuf.at[s, k - 1], p1s.at[s, k - 1], p1r.at[s, k - 1],
+            lbuf.at[lax.rem(y + k, ROW)], xbuf.at[k - 1], p1s.at[k - 1], p1r.at[k - 1],
             device_id=along_y(k), device_id_type=MESH)
 
-    def p2(s, k):
+    def p2(k):
         return pltpu.make_async_remote_copy(
-            rsend.at[s], zbuf.at[s, k - 1], p2s.at[s, k - 1], p2r.at[s, k - 1],
+            rsend, zbuf.at[k - 1], p2s.at[k - 1], p2r.at[k - 1],
             device_id=along_z(k), device_id_type=MESH)
 
-    def p3(s, k):
+    def p3(k):
         return pltpu.make_async_remote_copy(
-            esend.at[s, k - 1], ebuf.at[s, y], p3s.at[s, k - 1], p3r.at[s, k - 1],
+            esend.at[k - 1], ebuf.at[y], p3s.at[k - 1], p3r.at[k - 1],
             device_id=along_y(k), device_id_type=MESH)
 
-    def p3_in(s, k):
+    def p3_in(k):
         return pltpu.make_async_remote_copy(
-            esend.at[s, k - 1], ebuf.at[s, lax.rem(y - k + ROW, ROW)], p3s.at[s, k - 1], p3r.at[s, k - 1],
+            esend.at[k - 1], ebuf.at[lax.rem(y - k + ROW, ROW)], p3s.at[k - 1], p3r.at[k - 1],
             device_id=along_y(k), device_id_type=MESH)
 
-    def ss(s, k):
+    def ss(k):
         return pltpu.make_async_remote_copy(
-            ssb.at[s], ssr.at[s, k - 1], sss.at[s, k - 1], ssrs.at[s, k - 1],
+            ssb, ssr.at[k - 1], sss.at[k - 1], ssrs.at[k - 1],
             device_id=along_h(k), device_id_type=MESH)
 
     rowbase = z * (ROW * T)
+    owners = [y] + [lax.rem(y - k + ROW, ROW) for k in (1, 2, 3)]
 
     def last_of(j):
         return rowbase + (j + 1) * T - 1
 
     def gathered(s):
-        parts = [lbuf[s, y].astype(f32)]
-        owners = [y]
+        return [lbuf[y, s].astype(f32)] + [xbuf[k - 1, s].astype(f32) for k in (1, 2, 3)]
+
+    def row_sum():
+        keep = []
+        for s in range(2):
+            begin = begin_of(s, last_of(ROW - 1))
+            keep.append([begin <= last_of(j) for j in owners])
         for k in (1, 2, 3):
-            parts.append(xbuf[s, k - 1].astype(f32))
-            owners.append(lax.rem(y - k + ROW, ROW))
-        return parts, owners
-
-    def row_sum(s):
-        for k in (1, 2, 3):
-            p1(s, k).wait_recv()
-        parts, owners = gathered(s)
-        begin = begin_of(s, last_of(ROW - 1))
-        total = jnp.zeros((PIECE, HEAD), f32)
-        for part, j in zip(parts, owners):
-            total = total + jnp.where(begin <= last_of(j), part, 0.0)
-        rsend[s] = total.astype(bf16)
-        for k in (1, 2):
-            p2(s, k).start()
-
-    def entering(s):
-        for k in (1, 2):
-            p2(s, k).wait_recv()
-        parts, owners = gathered(s)
-        one, two = zbuf[s, 0].astype(f32), zbuf[s, 1].astype(f32)
+            p1(k).wait_recv()
+        for s in range(2):
+            total = jnp.zeros((PIECE, HEAD), f32)
+            for part, on in zip(gathered(s), keep[s]):
+                total = total + jnp.where(on, part, 0.0)
+            rsend[s] = total.astype(bf16)
+        for k in (2, 1):
+            p2(k).start()
         for k in (1, 2, 3, 0):
             target = lax.rem(y + k, ROW)
-            begin = begin_of(s, rowbase + target * T)
-            total = jnp.where(begin < rowbase, one, 0.0) + jnp.where(begin < rowbase - ROW * T, two, 0.0)
-            for part, j in zip(parts, owners):
-                reach = jnp.where(j < target, last_of(j), -1)
-                total = total + jnp.where(begin <= reach, part, 0.0)
+            for s in range(2):
+                begin = begin_of(s, rowbase + target * T)
+                total = jnp.zeros((PIECE, HEAD), f32)
+                for part, j in zip(gathered(s), owners):
+                    reach = jnp.where(j < target, last_of(j), -1)
+                    total = total + jnp.where(begin <= reach, part, 0.0)
+                inrow[k, s] = total
+
+    def entering():
+        reach = {}
+        for k in range(4):
+            target = lax.rem(y + k, ROW)
+            for s in range(2):
+                begin = begin_of(s, rowbase + target * T)
+                reach[k, s] = (begin < rowbase, begin < rowbase - ROW * T)
+        for k in (1, 2):
+            p2(k).wait_recv()
+        for k in (2, 1, 3, 0):
+            for s in range(2):
+                near, far = reach[k, s]
+                total = inrow[k, s] + jnp.where(near, zbuf[0, s].astype(f32), 0.0)
+                total = (total + jnp.where(far, zbuf[1, s].astype(f32), 0.0)).astype(bf16)
+                if k:
+                    esend[k - 1, s] = total
+                else:
+                    ebuf[y, s] = total
             if k:
-                esend[s, k - 1] = total.astype(bf16)
-                p3(s, k).start()
-            else:
-                ebuf[s, y] = total.astype(bf16)
+                p3(k).start()
 
     def attend(s, h):
         g = 2 * s + h
@@ -338,13 +349,15 @@
         for h in range(2):
             kk[2 * s + h] = nn(mk[h], qkt[s]).astype(bf16)
 
+    def entered():
+        for k in (1, 2, 3):
+            p3_in(k).wait_recv()
+
     def finish(s):
-        for k in (1, 2, 3):
-            p3_in(s, k).wait_recv()
         rhs = []
         f, l = iota((KEPT, HEAD), 0), iota((KEPT, HEAD), 1)
         for h in range(2):
-            state = jnp.concatenate([ebuf[s, 2 * h], ebuf[s, 2 * h + 1]], axis=0)
+            state = jnp.concatenate([ebuf[2 * h, s], ebuf[2 * h + 1, s]], axis=0)
             wide = state.astype(f32)
             n0, n1 = wide[ZROW:ZROW + 1], wide[ZROW + 1:ZROW + 2]
             norm = jnp.sum(jnp.where(f == l, n0, 0.0) + jnp.where(f == l + HEAD, n1, 0.0), axis=1, keepdims=True)
@@ -367,34 +380,37 @@
             col = jnp.sum(squares, axis=1, keepdims=True)
             i = r0 // 128
             ssb[s, i:i + 1, :] = jnp.sum(jnp.where(eye, col, 0.0), axis=0, keepdims=True)
+
+    peers = sorted(range(1, hn), key=lambda k: -min(k, hn - k))
+
+    def squares_out():
+        for k in peers:
+            ss(k).start()
+
+    def scale():
+        for k in peers:
+            ss(k).wait_recv()
+        total = ssb[...]
         for k in range(1, hn):
-            ss(s, k).start()
-
-    def scale(s):
-        for k in range(1, hn):
-            ss(s, k).wait_recv()
-        total = ssb[s]
-        for k in range(1, hn):
-            total = total + ssr[s, k - 1]
-        fac[s] = lax.rsqrt(total / (hn * 2 * HEAD) + 1e-06)
+            total = total + ssr[k - 1]
+        fac[...] = lax.rsqrt(total / (hn * 2 * HEAD) + 1e-06)
 
     def greet():
         pl.semaphore_wait(barrier, len(sources))
 
-    def pieces_out(s):
-        for k in (1, 2, 3):
-            p1(s, k).start()
+    def pieces_out():
+        for k in (2, 1, 3):
+            p1(k).start()
 
     def drain():
         rim.wait_send()
-        for s in range(2):
-            for k in (1, 2, 3):
-                p1(s, k).wait_send()
-                p3(s, k).wait_send()
-            for k in (1, 2):
-                p2(s, k).wait_send()
-            for k in range(1, hn):
-                ss(s, k).wait_send()
+        for k in (1, 2, 3):
+            p1(k).wait_send()
+            p3(k).wait_send()
+        for k in (1, 2):
+            p2(k).wait_send()
+        for k in peers:
+            ss(k).wait_send()
 
     L = C - 1
     plan = [(bounds,), (prepare,), (columns_in,)] + [(request, 0, c) for c in range(L)]
@@ -403,12 +419,11 @@
     plan += [(arrive, 0, c) for c in range(L)] + [(project, 0, 0, L)]
     plan += [(arrive, 1, c) for c in range(L)] + [(project, 1, 0, L)]
     plan += [(mix, 0, c) for c in range(1, C)] + [(mix, 1, c) for c in range(1, C)]
-    plan += [(rim_in,), (mix, 0, 0), (summarise, 0, 0), (summarise, 0, 1), (pieces_out, 0)]
-    plan += [(mix, 1, 0), (summarise, 1, 0), (summarise, 1, 1), (pieces_out, 1)]
-    plan += [(ready,), (turn, 0), (turn, 1), (attend, 0, 0)]
-    plan += [(row_sum, 0), (row_sum, 1), (attend, 0, 1), (attend, 1, 0)]
-    plan += [(entering, 0), (entering, 1), (queries, 0, 0), (queries, 0, 1), (queries, 1, 0), (queries, 1, 1)]
-    plan += [(attend, 1, 1), (finish, 0), (finish, 1), (scale, 0), (scale, 1), (drain,)]
+    plan += [(rim_in,), (mix, 0, 0), (summarise, 0, 0), (summarise, 0, 1)]
+    plan += [(mix, 1, 0), (summarise, 1, 0), (summarise, 1, 1), (pieces_out,)]
+    plan += [(ready,), (turn, 0), (turn, 1), (attend, 0, 0), (row_sum,), (attend, 0, 1), (attend, 1, 0), (entering,)]
+    plan += [(queries, s, h) for s in range(2) for h in range(2)] + [(attend, 1, 1), (entered,)]
+    plan += [(finish, 0), (finish, 1), (squares_out,), (scale,), (drain,)]
     for step, *where in plan:
         step(*where)
 
@@ -472,26 +487,27 @@
             pltpu.VMEM((4, T, 256), f32),
             pltpu.VMEM((2, RIM, 2 * WIDTH), bf16),
             pltpu.VMEM((2, RIM, 2 * WIDTH), bf16),
-            pltpu.VMEM((2, ROW, PIECE, HEAD), bf16),
-            pltpu.VMEM((2, 3, PIECE, HEAD), bf16),
+            pltpu.VMEM((ROW, 2, PIECE, HEAD), bf16),
+            pltpu.VMEM((3, 2, PIECE, HEAD), bf16),
             pltpu.VMEM((2, PIECE, HEAD), bf16),
             pltpu.VMEM((2, 2, PIECE, HEAD), bf16),
-            pltpu.VMEM((2, 3, PIECE, HEAD), bf16),
-            pltpu.VMEM((2, ROW, PIECE, HEAD), bf16),
+            pltpu.VMEM((3, 2, PIECE, HEAD), bf16),
+            pltpu.VMEM((ROW, 2, PIECE, HEAD), bf16),
+            pltpu.VMEM((4, 2, PIECE, HEAD), f32),
             pltpu.VMEM((2, T // 128, 128), f32),
-            pltpu.VMEM((2, max(hn - 1, 1), T // 128, 128), f32),
+            pltpu.VMEM((hn - 1, 2, T // 128, 128), f32),
             dma,
             dma((4,)),
             dma((2, C)),
             dma((2,)),
-            dma((2, 3)),
-            dma((2, 3)),
-            dma((2, 2)),
-            dma((2, 2)),
-            dma((2, 3)),
-            dma((2, 3)),
-            dma((2, max(hn - 1, 1))),
-            dma((2, max(hn - 1, 1))),
+            dma((3,)),
+            dma((3,)),
+            dma((2,)),
+            dma((2,)),
+            dma((3,)),
+            dma((3,)),
+            dma((hn - 1,)),
+            dma((hn - 1,)),
         ],
         compiler_params=pltpu.CompilerParams(
             collective_id=0, has_side_effects=True, vmem_limit_bytes=44 * 1024 * 1024),

time: 35 us -> 35.3 us (level)
  no operation moved by 1% of the time
where the time goes in v5:
time: 35.3 us; the launch traced here: 35.2 us
  Pallas kernels  35.2 us (100%)
    pallas_call x1, Pallas kernels, shards(): pl.pallas_call(functools.partial(kernel, zn, hn), out_shape=(jax.ShapeDty...  34.1 us
    pallas_call x1, Pallas kernels, shards(): pl.pallas_call(rescale, out_shape=jax.ShapeDtypeStruct((seqs, T, 2 * HEAD...  1.14 us

profile of v5, /device:TPU:1, one launch (start us, length us, event | category | flops | bytes accessed | tf_op | source)
XLA Modules:
  0.0 35.2 jit_solution(14777607922159941465)
XLA Ops:
  0.0 0.0 copy-start
  0.0 34.1 %packed_linear_attention.1 = (f32[2,1024,256]{2,1,0:T(8,128)S(1)}, f32[2,8,128]{2,1,0:T(8,128)S(1)}) custom-call(bf16[2,1024,2048]{2,1,0:T(8,128)(2,1)} %hid.1, bf16[320,2048]{1,0:T(8,128)(2,1)} %bitcast.1, f32[3,320]{1,0:T(4,128)} %conv_in.1, s32[2,12]{1,0:T(2,128)} %lengths_in.1, bf16[2,128,512]{2,1,0:T(8,128)(2,1)} %constant.4.clone.eq_in, ...), custom_call_target="tpu_custom_call" | custom-call | tf_op jit(solution)/shard_map/packed_linear_attention/pallas_call | solution.py:464
  34.1 0.0 copy-done
  34.1 1.1 %rescale_rows.1 = bf16[2,1024,256]{2,1,0:T(8,128)(2,1)} custom-call(f32[2,1024,256]{2,1,0:T(8,128)S(1)} %get-tuple-element.7.att, f32[2,8,128]{2,1,0:T(8,128)S(1)} %get-tuple-element.8.fac, bf16[256]{0:T(256)(128)(2,1)S(1)} %copy-done), custom_call_target="tpu_custom_call" | custom-call | tf_op jit(solution)/shard_map/rescale_rows/pallas_call | solution.py:516
Async XLA Ops:
  0.0 34.1 %copy-start = (bf16[256]{0:T(256)(128)(2,1)S(1)}, bf16[256]{0:T(256)(128)(2,1)}, u32[]{:S(2)}) copy-start(bf16[256]{0:T(256)(128)(2,1)} %gain.1) | copy-start | bytes 1540

commit v6 on v5

--- a/solution.py
+++ b/solution.py
@@ -180,20 +180,20 @@
             qkv[s, :, 0:128] = lax.dot_general(
                 rim_r[s], pick, (((0,), (0,)), ((), ())), preferred_element_type=f32)
 
-    def mix(s, c):
-        lanes = slice(c * CHUNK, (c + 1) * CHUNK)
+    def mix(s, low, high):
+        lanes = slice(low, high)
         first = jnp.concatenate([lor[s, :, lanes]] * 4, axis=0)
-        pos = c * CHUNK + iota((32, CHUNK), 1)
+        pos = low + iota((32, high - low), 1)
         one_back = first < pos
         two_back = first < pos - 1
         for r0 in range(0, 2 * WIDTH, 32):
             rows = slice(r0, r0 + 32)
-            ext = qkv[s, rows, c * CHUNK:(c + 1) * CHUNK + 128]
+            ext = qkv[s, rows, low:high + 128]
             x1 = pltpu.roll(ext, 1, 1)[:, 128:]
             x2 = pltpu.roll(ext, 2, 1)[:, 128:]
 
             def tap(j):
-                return jnp.concatenate([taps[j, rows, :]] * (CHUNK // 128), axis=1)
+                return jnp.concatenate([taps[j, rows, :]] * ((high - low) // 128), axis=1)
 
             m = tap(0) * ext[:, 128:]
             m = m + tap(1) * jnp.where(one_back, x1, 0.0)
@@ -205,11 +205,10 @@
             else:
                 vv[2 * s + h, d - 32:d, lanes] = m
 
-    def summarise(s, half):
+    def summarise(s, at, until):
         inside = begin_of(s, base + T - 1) - base
-        W = T // 2
-        at = half * W
-        lanes = slice(at, at + W)
+        W = until - at
+        lanes = slice(at, until)
         for h in range(2):
             g = 2 * s + h
             key = qkt[s, 32 * h + FEAT:32 * h + 2 * FEAT, lanes].astype(f32)
@@ -223,7 +222,7 @@
             blocks.append(jnp.concatenate(last, axis=0).astype(bf16))
             blocks.append((key * 0.125).astype(bf16))
             total = nt(jnp.concatenate(blocks, axis=0), vv[g, :, lanes])
-            if half == 0:
+            if at:
                 partial[g] = total
                 continue
             total = partial[g] + total
@@ -418,9 +417,11 @@
     plan += [(project, 0, L, C), (project, 1, L, C), (greet,), (rim.start,)]
     plan += [(arrive, 0, c) for c in range(L)] + [(project, 0, 0, L)]
     plan += [(arrive, 1, c) for c in range(L)] + [(project, 1, 0, L)]
-    plan += [(mix, 0, c) for c in range(1, C)] + [(mix, 1, c) for c in range(1, C)]
-    plan += [(rim_in,), (mix, 0, 0), (summarise, 0, 0), (summarise, 0, 1)]
-    plan += [(mix, 1, 0), (summarise, 1, 0), (summarise, 1, 1), (pieces_out,)]
+    cuts = [128] + [c * CHUNK for c in range(1, C + 1)]
+    for s in range(2):
+        plan += [(mix, s, low, high) for low, high in zip(cuts, cuts[1:])] + [(summarise, s, 128, T)]
+    plan += [(rim_in,), (mix, 0, 0, 128), (mix, 1, 0, 128)]
+    plan += [(summarise, 0, 0, 128), (summarise, 1, 0, 128), (pieces_out,)]
     plan += [(ready,), (turn, 0), (turn, 1), (attend, 0, 0), (row_sum,), (attend, 0, 1), (attend, 1, 0), (entering,)]
     plan += [(queries, s, h) for s in range(2) for h in range(2)] + [(attend, 1, 1), (entered,)]
     plan += [(finish, 0), (finish, 1), (squares_out,), (scale,), (drain,)]

time: 35.3 us -> 34.9 us (0.989)
  Pallas kernels: 35.2 us -> 34.8 us
    pallas_call x1, Pallas kernels: 34.1 us -> 33.7 us  [shards(): pl.pallas_call(functools.partial(kernel, zn, hn), out_shape=(jax.ShapeDty...]
where the time goes in v6:
time: 34.9 us; the launch traced here: 34.8 us
  Pallas kernels  34.8 us (100%)
    pallas_call x1, Pallas kernels, shards(): pl.pallas_call(functools.partial(kernel, zn, hn), out_shape=(jax.ShapeDty...  33.7 us
    pallas_call x1, Pallas kernels, shards(): pl.pallas_call(rescale, out_shape=jax.ShapeDtypeStruct((seqs, T, 2 * HEAD...  1.14 us

profile of v6, /device:TPU:1, one launch (start us, length us, event | category | flops | bytes accessed | tf_op | source)
XLA Modules:
  0.0 34.8 jit_solution(8429171825472915398)
XLA Ops:
  0.0 0.0 copy-start
  0.0 33.7 %packed_linear_attention.1 = (f32[2,1024,256]{2,1,0:T(8,128)S(1)}, f32[2,8,128]{2,1,0:T(8,128)S(1)}) custom-call(bf16[2,1024,2048]{2,1,0:T(8,128)(2,1)} %hid.1, bf16[320,2048]{1,0:T(8,128)(2,1)} %bitcast.1, f32[3,320]{1,0:T(4,128)} %conv_in.1, s32[2,12]{1,0:T(2,128)} %lengths_in.1, bf16[2,128,512]{2,1,0:T(8,128)(2,1)} %constant.4.clone.eq_in, ...), custom_call_target="tpu_custom_call" | custom-call | tf_op jit(solution)/shard_map/packed_linear_attention/pallas_call | solution.py:465
  33.7 0.0 copy-done
  33.7 1.1 %rescale_rows.1 = bf16[2,1024,256]{2,1,0:T(8,128)(2,1)} custom-call(f32[2,1024,256]{2,1,0:T(8,128)S(1)} %get-tuple-element.7.att, f32[2,8,128]{2,1,0:T(8,128)S(1)} %get-tuple-element.8.fac, bf16[256]{0:T(256)(128)(2,1)S(1)} %copy-done), custom_call_target="tpu_custom_call" | custom-call | tf_op jit(solution)/shard_map/rescale_rows/pallas_call | solution.py:517
Async XLA Ops:
  0.0 33.7 %copy-start = (bf16[256]{0:T(256)(128)(2,1)S(1)}, bf16[256]{0:T(256)(128)(2,1)}, u32[]{:S(2)}) copy-start(bf16[256]{0:T(256)(128)(2,1)} %gain.1) | copy-start | bytes 1540

commit v7 on v6

--- a/solution.py
+++ b/solution.py
@@ -422,7 +422,7 @@
         plan += [(mix, s, low, high) for low, high in zip(cuts, cuts[1:])] + [(summarise, s, 128, T)]
     plan += [(rim_in,), (mix, 0, 0, 128), (mix, 1, 0, 128)]
     plan += [(summarise, 0, 0, 128), (summarise, 1, 0, 128), (pieces_out,)]
-    plan += [(ready,), (turn, 0), (turn, 1), (attend, 0, 0), (row_sum,), (attend, 0, 1), (attend, 1, 0), (entering,)]
+    plan += [(ready,), (turn, 0), (turn, 1), (row_sum,), (attend, 0, 0), (attend, 0, 1), (entering,), (attend, 1, 0)]
     plan += [(queries, s, h) for s in range(2) for h in range(2)] + [(attend, 1, 1), (entered,)]
     plan += [(finish, 0), (finish, 1), (squares_out,), (scale,), (drain,)]
     for step, *where in plan:

time: 34.9 us -> 34.9 us (level)
  no operation moved by 1% of the time
where the time goes in v7:
time: 34.9 us; the launch traced here: 34.8 us
  Pallas kernels  34.8 us (100%)
    pallas_call x1, Pallas kernels, shards(): pl.pallas_call(functools.partial(kernel, zn, hn), out_shape=(jax.ShapeDty...  33.7 us
    pallas_call x1, Pallas kernels, shards(): pl.pallas_call(rescale, out_shape=jax.ShapeDtypeStruct((seqs, T, 2 * HEAD...  1.14 us

profile of v7, /device:TPU:1, one launch (start us, length us, event | category | flops | bytes accessed | tf_op | source)
XLA Modules:
  0.0 34.8 jit_solution(7677108382744200013)
XLA Ops:
  0.0 0.0 copy-start
  0.0 33.7 %packed_linear_attention.1 = (f32[2,1024,256]{2,1,0:T(8,128)S(1)}, f32[2,8,128]{2,1,0:T(8,128)S(1)}) custom-call(bf16[2,1024,2048]{2,1,0:T(8,128)(2,1)} %hid.1, bf16[320,2048]{1,0:T(8,128)(2,1)} %bitcast.1, f32[3,320]{1,0:T(4,128)} %conv_in.1, s32[2,12]{1,0:T(2,128)} %lengths_in.1, bf16[2,128,512]{2,1,0:T(8,128)(2,1)} %constant.4.clone.eq_in, ...), custom_call_target="tpu_custom_call" | custom-call | tf_op jit(solution)/shard_map/packed_linear_attention/pallas_call | solution.py:465
  33.7 0.0 copy-done
  33.7 1.1 %rescale_rows.1 = bf16[2,1024,256]{2,1,0:T(8,128)(2,1)} custom-call(f32[2,1024,256]{2,1,0:T(8,128)S(1)} %get-tuple-element.7.att, f32[2,8,128]{2,1,0:T(8,128)S(1)} %get-tuple-element.8.fac, bf16[256]{0:T(256)(128)(2,1)S(1)} %copy-done), custom_call_target="tpu_custom_call" | custom-call | tf_op jit(solution)/shard_map/rescale_rows/pallas_call | solution.py:517
Async XLA Ops:
  0.0 33.7 %copy-start = (bf16[256]{0:T(256)(128)(2,1)S(1)}, bf16[256]{0:T(256)(128)(2,1)}, u32[]{:S(2)}) copy-start(bf16[256]{0:T(256)(128)(2,1)} %gain.1) | copy-start | bytes 1540
